TPU v7x, 32 devices: a whole 2x2x4 slice. The times are simulated.
32 devices in a mesh: ifg: 16 (over z, y, x), tile: 2 (over core).
Axes of the slice: x: 2, y: 2, z: 4, core: 2. Of those that a mesh axis runs over, the one named last changes fastest.
Arguments:
- phases: float32 [1024, 128, 64], P('ifg', 'tile'), may hold values from -6 to 6
- pairs: int32 [1024, 2], replicated, may hold values from 0 to 299, as said below
- class_weights: float32 [8, 1024], replicated, may hold values from 0.05 to 1
- classes: int32 [128, 64], P('tile', 'ifg'), may hold values from 0 to 7
Outputs:
- corrected: float32 [128, 64, 300], P('tile', 'ifg')
Inputs may be any that keep to these rules, and one draw needn't show every extreme that they name: pairs[i,0] < pairs[i,1] <= pairs[i,0] + 8; some interferogram starts at date 0 and some ends at date 300 - 1.
All inputs are finite; a program needn't handle non-finite values.
Results may differ from a plain program's by a relative error of at most 0.0003.
Values sent between devices are 32-bit elements; how exact they have to be, the bound alone decides.
A program may use at most 128 MiB of HBM per device.

v0:
```python
import jax
import jax.numpy as jnp
from jax import lax
from jax.sharding import PartitionSpec as P

DATES = 300
CLASSES = 8
MAXGAP = 8
R = 3


smooth_weight = 1.0
anchor_weight = 0.1


def with_halo(cells, sides, width):
    for axis, dim in sides:
        count = lax.axis_size(axis)
        ends = count - 1
        head = lax.slice_in_dim(cells, 0, width, axis=dim)
        tail = lax.slice_in_dim(cells, cells.shape[dim] - width, cells.shape[dim], axis=dim)
        cells = jnp.concatenate(
            [
                lax.ppermute(tail, axis, [(i, (i + 1) % count) for i in range(ends)]),
                cells,
                lax.ppermute(head, axis, [((i + 1) % count, i) for i in range(ends)]),
            ],
            axis=dim,
        )
    return cells


def incidence_matrix(pairs):
    dates = jnp.arange(DATES, dtype=jnp.int32)[:, None]
    plus = (dates == pairs[:, 1][None, :]).astype(jnp.float32)
    minus = (dates == pairs[:, 0][None, :]).astype(jnp.float32)
    return (plus, minus)


def prior_matrix():
    second = jnp.arange(DATES - 2, dtype=jnp.int32)[:, None]
    columns = jnp.arange(DATES, dtype=jnp.int32)[None, :]
    diffs = (
        (columns == second).astype(jnp.float32)
        - 2.0 * (columns == second + 1).astype(jnp.float32)
        + (columns == second + 2).astype(jnp.float32)
    )
    curvature = jnp.dot(
        diffs.T, diffs, precision=lax.Precision.HIGHEST, preferred_element_type=jnp.float32
    )
    return smooth_weight * curvature + anchor_weight * jnp.eye(DATES, dtype=jnp.float32)


def class_systems(pairs, plus, minus, weights):
    diagonal = jnp.dot(
        weights,
        (plus + minus).T,
        precision=lax.Precision.HIGHEST,
        preferred_element_type=jnp.float32,
    )
    spacing = pairs[:, 1] - pairs[:, 0]
    offsets = jnp.arange(1, MAXGAP + 1, dtype=jnp.int32)[:, None]
    gap_onehot = (spacing[None, :] == offsets).astype(jnp.float32)
    spread = weights[:, None, :] * gap_onehot[None, :, :]
    band = jnp.einsum("kgi,ai->kga", spread, minus, precision=lax.Precision.HIGHEST)
    row_ids = jnp.arange(DATES, dtype=jnp.int32)[:, None]
    col_ids = jnp.arange(DATES, dtype=jnp.int32)[None, :]
    normal = diagonal[:, :, None] * (row_ids == col_ids).astype(jnp.float32)[None]
    for offset in range(MAXGAP):
        select = (col_ids == row_ids + offset + 1).astype(jnp.float32)
        normal = (
            normal
            - band[:, offset, :, None] * select[None]
            - band[:, offset, None, :] * select.T[None]
        )
    return normal


def invert(matrix):
    factor = jnp.linalg.cholesky(matrix)
    return jax.scipy.linalg.cho_solve((factor, True), jnp.eye(DATES, dtype=jnp.float32))


def filter_taps():
    offsets = jnp.arange(-R, R + 1).astype(jnp.float32)
    values = jnp.exp(-offsets * offsets / 4.5)
    return values / jnp.sum(values)


def pass_columns(padded, filter_weights, width):
    result = filter_weights[0] * padded[:, 0:width]
    for offset in range(1, 2 * R + 1):
        result = result + filter_weights[offset] * padded[:, offset : offset + width]
    return result


def pass_rows(padded, filter_weights, height):
    result = filter_weights[0] * padded[0:height]
    for offset in range(1, 2 * R + 1):
        result = result + filter_weights[offset] * padded[offset : offset + height]
    return result


def date_terms(received, incidence, weight_rows, onehot):
    flat = received.reshape(received.shape[0], -1)
    pixel_weights = jnp.dot(
        weight_rows, onehot, precision=lax.Precision.HIGHEST, preferred_element_type=jnp.float32
    )
    return jnp.einsum("ip,di->pd", pixel_weights * flat, incidence, precision=lax.Precision.HIGHEST)


def on_device(phases, pairs, class_weights, classes):
    plus, minus = incidence_matrix(pairs)
    incidence = plus - minus
    class_share = CLASSES // lax.axis_size("tile")
    first_class = lax.axis_index("tile") * class_share
    own_weights = lax.dynamic_slice_in_dim(class_weights, first_class, class_share, 0)
    own_normal = class_systems(pairs, plus, minus, own_weights)
    own_inverse = jax.vmap(invert)(own_normal + prior_matrix()[None])
    inverse = lax.all_gather(own_inverse, "tile", axis=0, tiled=True)
    tile_rows = phases.shape[1]
    tile_cols = classes.shape[1]
    class_flat = classes.reshape(-1)
    onehot = (class_flat[None, :] == jnp.arange(CLASSES, dtype=jnp.int32)[:, None]).astype(
        jnp.float32
    )
    weight_rows = class_weights.T
    regrouped = lax.all_to_all(phases, "ifg", split_axis=2, concat_axis=0, tiled=True)
    right_terms = date_terms(regrouped, incidence, weight_rows, onehot)
    solution = jnp.zeros((tile_rows * tile_cols, DATES), jnp.float32)
    for member in range(CLASSES):
        solved = jnp.einsum(
            "pd,ed->pe", right_terms, inverse[member], precision=lax.Precision.HIGHEST
        )
        solution = solution + onehot[member][:, None] * solved
    displacement = solution.reshape(tile_rows, tile_cols, DATES)
    filter_weights = filter_taps()
    padded = with_halo(displacement, (("ifg", 1), ("tile", 0)), R)
    across = pass_columns(padded, filter_weights, tile_cols)
    atmosphere = pass_rows(across, filter_weights, tile_rows)
    return displacement - atmosphere


def solution(mesh):
    return jax.shard_map(
        on_device,
        mesh=mesh,
        in_specs=(P("ifg", "tile", None), P(), P(), P("tile", "ifg")),
        out_specs=P("tile", "ifg", None),
        check_vma=False,
    )
```

profile of v0, /device:TPU:1, one launch (start us, length us, event | category | flops | bytes accessed | tf_op | source)
XLA Modules:
  0.0 463.3 jit_solution(6404731645494615155)
XLA Ops:
  7.3 1.3 fusion.6
  8.7 0.7 fusion.15
  9.5 1.4 bitcast_add_fusion
  12.6 4.5 fusion.2
  17.2 1.3 copy-done.2
  18.4 46.9 %custom-call.29 = f32[4,128,128]{2,1,0:T(8,128)S(1)} custom-call(f32[4,128,128]{2,1,0:T(8,128)S(1)} %cholesky.205), custom_call_target="Cholesky" | custom-call | tf_op jit(solution)/shard_map/vmap(jit(cholesky))/cholesky | solution.py:80
  65.5 39.9 %custom-call.30 = f32[4,1,128,128]{2,3,1,0:T(8,128)} custom-call(f32[4,1,128,128]{3,2,1,0:T(8,128)S(1)} %select_bitcast_fusion.1), custom_call_target="InvertDiagBlocksLowerTriangular" | custom-call | tf_op jit(solution)/shard_map/vmap(jit(cholesky))/cholesky | solution.py:80
  105.4 1.5 constant_dynamic-update-slice_fusion.2
  107.0 1.7 convolution_subtract_fusion.3
  108.6 0.7 cholesky.209
  109.4 48.6 %custom-call.31 = f32[4,128,128]{2,1,0:T(8,128)} custom-call(f32[4,128,128]{2,1,0:T(8,128)} %cholesky.209), custom_call_target="Cholesky" | custom-call | tf_op jit(solution)/shard_map/vmap(jit(cholesky))/cholesky | solution.py:80
  157.9 1.7 select_reduce_fusion
  159.6 40.1 %custom-call.32 = f32[4,1,128,128]{2,3,1,0:T(8,128)S(1)} custom-call(f32[4,1,128,128]{3,2,1,0:T(8,128)} %get-tuple-element.31), custom_call_target="InvertDiagBlocksLowerTriangular" | custom-call | tf_op jit(solution)/shard_map/vmap(jit(cholesky))/cholesky | solution.py:80
  200.1 1.2 convolution_subtract_fusion.4
  201.3 16.1 %custom-call.33 = f32[4,44,44]{2,1,0:T(8,128)S(1)} custom-call(f32[4,44,44]{2,1,0:T(8,128)S(1)} %convolution_subtract_fusion.4), custom_call_target="Cholesky" | custom-call | tf_op jit(solution)/shard_map/vmap(jit(cholesky))/cholesky | solution.py:80
  217.9 0.9 copy-done.1
  218.8 1.8 select_select_fusion
  220.6 4.1 while.1
  220.7 0.6 fusion.131
  221.2 1.4 bitcast_dynamic-update-slice_fusion.2
  222.7 0.6 fusion.131
  223.3 1.4 bitcast_dynamic-update-slice_fusion.2
  225.0 119.0 %custom-call.34 = f32[4,3,128,128]{2,3,1,0:T(8,128)} custom-call(f32[4,3,128,128]{3,2,1,0:T(8,128)S(1)} %pad_maximum_fusion.2), custom_call_target="InvertDiagBlocksLowerTriangular" | custom-call | tf_op jit(solution)/shard_map/vmap(jit(_cho_solve))/triangular_solve | solution.py:81
  344.0 1.6 fusion.72
  345.6 0.7 convolution_subtract_fusion
  346.3 1.6 fusion.81
  348.1 1.3 fusion.24
  349.3 1.3 fusion.92
  350.7 1.3 fusion.91
  352.0 2.0 convolution_subtract_fusion.1
  354.2 1.8 fusion.80
  356.1 1.2 convolution_subtract_fusion.2
  357.3 1.6 fusion.79
  359.0 1.8 copy.89
  360.9 3.1 copy.69
  364.0 2.3 reshape.539
  366.3 7.6 %all-to-all-start = ((f32[16,1,16384]{2,1,0:T(1,128)}), f32[16,1,16384]{2,1,0:T(1,128)S(1)}, u32[]{:S(2)}, u32[]{:S(2)}) async-start(f32[16,1,16384]{2,1,0:T(1,128)} %reshape.539), calls=%async_computation | async-start | bytes 2097152 | tf_op jit(solution)/shard_map/all_to_all | solution.py:128
  374.1 22.0 %all-to-all-done = f32[16,1,16384]{2,1,0:T(1,128)S(1)} async-done(((f32[16,1,16384]{2,1,0:T(1,128)}), f32[16,1,16384]{2,1,0:T(1,128)S(1)}, u32[]{:S(2)}, u32[]{:S(2)}) %all-to-all-start) | async-done | bytes 1048608 | tf_op jit(solution)/shard_map/all_to_all | solution.py:128
  396.1 0.5 broadcast.592
  396.6 3.1 reduce.18
  399.7 0.8 reshape.540
  400.6 2.7 copy.70
  403.3 2.0 reshape.515
  405.3 0.6 fusion.4
  405.9 1.4 fusion.5
  407.4 1.8 convolution_multiply_fusion.6
  409.2 1.7 convolution_multiply_fusion.5
  410.9 1.7 convolution_multiply_fusion.4
  412.6 1.7 convolution_multiply_fusion.3
  414.3 0.7 convolution_multiply_fusion.2
  415.0 0.7 convolution_multiply_fusion.1
  415.7 0.7 convolution_multiply_fusion
  416.3 0.7 fusion.23
  417.5 1.9 collective-permute-start
  419.4 1.3 collective-permute-start.1
  420.7 0.6 fusion.99
  421.3 0.7 broadcast_divide_fusion
  421.9 2.3 collective-permute-done
  424.3 13.2 %collective-permute-done.1 = f32[64,3,300]{2,1,0:T(4,128)S(1)} collective-permute-done((f32[64,3,300]{2,1,0:T(4,128)S(1)}, f32[64,3,300]{2,1,0:T(4,128)S(1)}, u32[]{:S(2)}, u32[]{:S(2)}) %collective-permute-start.1) | collective-permute-done | bytes 230432 | tf_op jit(solution)/shard_map/ppermute | solution.py:26
  437.5 1.3 collective-permute-start.2
  438.8 5.6 %collective-permute-start.3 = (f32[3,10,300]{2,1,0:T(8,128)S(1)}, f32[3,10,300]{2,1,0:T(8,128)S(1)}, u32[]{:S(2)}, u32[]{:S(2)}) collective-permute-start(f32[3,10,300]{2,1,0:T(8,128)S(1)} %get-tuple-element.26), channel_id=1, source_target_pairs={{1,0},{3,2},{5,4},{7,6},{9,8},{11,10},{13,12},{15,14},{17,16},{19,... | collective-permute-start | bytes 108008 | tf_op jit(solution)/shard_map/ppermute | solution.py:26
  444.4 0.7 fusion.110
  445.7 5.0 %fusion.56 = f32[70,4,300]{2,1,0:T(4,128)S(1)} fusion(f32[70,10,300]{2,1,0:T(8,128)S(1)} %pad_maximum_fusion.1, f32[]{:T(128)} %bitcast.39, f32[]{:T(128)} %bitcast.38, f32[]{:T(128)} %bitcast.37, f32[]{:T(128)} %bitcast.36, f32[]{:T(128)} %bitcast.35, f32[]{:T(128)} %bitcast.34, f32[]{:T(128)} %bitcast.33), kind=kLoop, calls=%fused_computation.143 | loop fusion | flops 1092000 | bytes 2688028 | tf_op jit(solution)/shard_map/add | solution.py:93
  450.8 5.5 %fusion.63 = f32[64,4,300]{2,1,0:T(4,128)} fusion(f32[64,4,300]{2,1,0:T(4,128)S(1)} %reshape.516, f32[70,4,300]{2,1,0:T(4,128)S(1)} %fusion.56, f32[]{:T(128)} %bitcast.39, f32[]{:T(128)} %bitcast.38, f32[]{:T(128)} %bitcast.37, f32[]{:T(128)} %bitcast.36, f32[]{:T(128)} %bitcast.35, f32[]{:T(128)} %bitcast.34, f32[]{:T(128)} %bitcast.33), kind=kLoop, calls=%fused_computation.157 | loop fusion | flops 1075200 | bytes 2764828 | tf_op jit(solution)/shard_map/sub | solution.py:141
  (86 shorter events, 5.5 us)
Async XLA Ops:
  6.5 0.8 copy-start
  6.5 0.7 copy-start.5
  6.5 400.8 %all-gather.2.cloned.1.call-start = ((), (), s32[]{:S(2)}) async-start(), calls=%async_computation.1 | async-start | bytes 5603328 | tf_op jit(solution)/shard_map/all_gather | solution.py:120
  6.7 2.7 copy-start.3
  17.2 1.3 copy-start.2
  217.5 1.3 copy-start.1
  344.0 4.0 slice-start
  364.0 9.9 %copy-start.6 = (s32[64,4]{0,1:T(4,128)S(1)}, s32[64,4]{0,1:T(4,128)}, u32[]{:S(2)}) copy-start(s32[64,4]{0,1:T(4,128)} %param.7) | copy-start | bytes 3076
  366.3 29.8 %all-to-all-start = ((f32[16,1,16384]{2,1,0:T(1,128)}), f32[16,1,16384]{2,1,0:T(1,128)S(1)}, u32[]{:S(2)}, u32[]{:S(2)}) async-start(f32[16,1,16384]{2,1,0:T(1,128)} %reshape.539), calls=%async_computation | async-start | bytes 2097152 | tf_op jit(solution)/shard_map/all_to_all | solution.py:128
  407.4 6.9 %copy-start.4 = (f32[8,300,300]{2,1,0:T(8,128)S(1)}, f32[8,300,300]{2,1,0:T(8,128)}, u32[]{:S(2)}) copy-start(f32[8,300,300]{2,1,0:T(8,128)} %all-gather.2.cloned.1.call-done) | copy-start | bytes 8640004
  417.5 6.8 %collective-permute-start = (f32[64,3,300]{2,1,0:T(4,128)S(1)}, f32[64,3,300]{2,1,0:T(4,128)S(1)}, u32[]{:S(2)}, u32[]{:S(2)}) collective-permute-start(f32[64,3,300]{2,1,0:T(4,128)S(1)} %get-tuple-element.29), channel_id=1, source_target_pairs={{0,2},{2,4},{4,6},{6,8},{8,10},{10,12},{12,14},{14,16},{16,18},{18... | collective-permute-start | bytes 691208 | tf_op jit(solution)/shard_map/ppermute | solution.py:24
  419.4 18.1 %collective-permute-start.1 = (f32[64,3,300]{2,1,0:T(4,128)S(1)}, f32[64,3,300]{2,1,0:T(4,128)S(1)}, u32[]{:S(2)}, u32[]{:S(2)}) collective-permute-start(f32[64,3,300]{2,1,0:T(4,128)S(1)} %get-tuple-element.30), channel_id=1, source_target_pairs={{2,0},{4,2},{6,4},{8,6},{10,8},{12,10},{14,12},{16,14},{18,16},{20... | collective-permute-start | bytes 691208 | tf_op jit(solution)/shard_map/ppermute | solution.py:26
  437.5 7.6 %collective-permute-start.2 = (f32[3,10,300]{2,1,0:T(8,128)S(1)}, f32[3,10,300]{2,1,0:T(8,128)S(1)}, u32[]{:S(2)}, u32[]{:S(2)}) collective-permute-start(f32[3,10,300]{2,1,0:T(8,128)S(1)} %get-tuple-element.25), channel_id=1, source_target_pairs={{0,1},{2,3},{4,5},{6,7},{8,9},{10,11},{12,13},{14,15},{16,17},{18,... | collective-permute-start | bytes 108008 | tf_op jit(solution)/shard_map/ppermute | solution.py:24
  438.8 6.5 %collective-permute-start.3 = (f32[3,10,300]{2,1,0:T(8,128)S(1)}, f32[3,10,300]{2,1,0:T(8,128)S(1)}, u32[]{:S(2)}, u32[]{:S(2)}) collective-permute-start(f32[3,10,300]{2,1,0:T(8,128)S(1)} %get-tuple-element.26), channel_id=1, source_target_pairs={{1,0},{3,2},{5,4},{7,6},{9,8},{11,10},{13,12},{15,14},{17,16},{19,... | collective-permute-start | bytes 108008 | tf_op jit(solution)/shard_map/ppermute | solution.py:26
Sparse Core Ops, SparseCore 0:
  361.0 15.4 all-gather.1
where the time goes:
time: 470 us; the launch traced here: 463 us
  other arithmetic  336 us (71%)
  waiting for transfers between devices  37.7 us (8%)
  matrix products  34.2 us (7%)
  local copies, waits for them, and re-layouts  23.4 us (5%)
  starting transfers between devices  17.7 us (4%)
  between operations  14.3 us (3%)
    another operation x14, other arithmetic, invert(): factor = jnp.linalg.cholesky(matrix)  194 us
    another operation x9, other arithmetic, invert(): jax.scipy.linalg.cho_solve((factor, True), jnp.eye(DATES, dtype=jnp.float...  121 us
    all_to_all x1, waiting for transfers between devices, on_device(): lax.all_to_all(phases, 'ifg', split_axis=2, concat_axis=0, tiled=True)  22 us
    another operation x10, matrix products, invert(): jax.scipy.linalg.cho_solve((factor, True), jnp.eye(DATES, dtype=jnp.float...  14.5 us
    ppermute x2, waiting for transfers between devices, with_halo(): lax.ppermute(head, axis, [((i + 1) % count, i) for i in range(ends)])  13.4 us
    dot_general x8, matrix products, on_device(): jnp.einsum('pd,ed->pe', right_terms, inverse[member], precision=lax.Preci...  9.61 us
  transfers between devices with their start and end apart: 6, of which 4 were waited for; matrix products, arithmetic and copies ran while one was open for 4% of the time, Pallas kernels for 0%

commit v1 on v0

v1 whole, which is shorter than its diff:
```python
import functools
import jax
import jax.numpy as jnp
from jax import lax
from jax.experimental import pallas as pl
from jax.experimental.pallas import tpu as pltpu
from jax.sharding import PartitionSpec as P

DATES = 300
CLASSES = 8
MAXGAP = 8
R = 3
LANES = 128
PAD = -(-DATES // 8) * 8
MESH = pl.DeviceIdType.MESH
HIGHEST = lax.Precision.HIGHEST

smooth_weight = 1.0
anchor_weight = 0.1


def split3(value):
    high = value.astype(jnp.bfloat16)
    rest = value - high.astype(jnp.float32)
    middle = rest.astype(jnp.bfloat16)
    low = (rest - middle.astype(jnp.float32)).astype(jnp.bfloat16)
    return (high, middle, low)


def dot_nt(a, b, **kw):
    return lax.dot_general(a, b, (((1,), (1,)), ((), ())), preferred_element_type=jnp.float32, **kw)


def dot_nn(a, b, **kw):
    return lax.dot_general(a, b, (((1,), (0,)), ((), ())), preferred_element_type=jnp.float32, **kw)


def factor_kernel(pairs_ref, w_ref, wt_ref, cls_ref, inc_ref, wpx_ref, lpx_ref, band, low):
    nifg = pairs_ref.shape[1]
    pixels = cls_ref.shape[1]
    first = pairs_ref[0:1, :]
    second = pairs_ref[1:2, :]
    gap = second - first
    dates = lax.broadcasted_iota(jnp.int32, (PAD, nifg), 0)
    minus_f = jnp.where(dates == first, 1.0, 0.0)
    plus_f = jnp.where(dates == second, 1.0, 0.0)
    inc_ref[...] = (plus_f - minus_f).astype(jnp.bfloat16)
    minus = minus_f.astype(jnp.bfloat16)
    both = (plus_f + minus_f).astype(jnp.bfloat16)
    w = w_ref[...]
    row = lax.broadcasted_iota(jnp.int32, (PAD, LANES), 0)
    inside = lambda ok: jnp.where(ok, 1.0, 0.0)
    for g in range(MAXGAP + 1):
        parts = split3(w if g == 0 else jnp.where(gap == g, w, 0.0))
        left = both if g == 0 else minus
        total = dot_nt(left, parts[0]) + (dot_nt(left, parts[1]) + dot_nt(left, parts[2]))
        here = inside(row <= DATES - 3)
        before = inside((row >= 1) & (row <= DATES - 2))
        if g == 0:
            twice = inside((row >= 2) & (row <= DATES - 1))
            prior = smooth_weight * (here + 4.0 * before + twice) + anchor_weight
            total = total + jnp.where(row < DATES, prior, 1.0)
        elif g == 1:
            total = smooth_weight * (-2.0 * here - 2.0 * before) - total
        elif g == 2:
            total = smooth_weight * here - total
        else:
            total = -total
        band[g] = total

    zero = jnp.zeros((1, LANES), jnp.float32)
    keys = [(j, h) for j in range(MAXGAP) for h in range(MAXGAP - j)]

    def factor_block(block, carry):
        acc = dict(zip(keys, carry))
        base = pl.multiple_of(block * 8, 8)
        for s in range(8):
            at = pl.ds(base + s, 1)
            c = [band[h, at, :] for h in range(MAXGAP + 1)]
            c = [c[h] - acc[(0, h)] for h in range(MAXGAP)] + [c[MAXGAP]]
            inv = 1.0 / c[0]
            low[0, at, :] = inv
            fresh = {}
            for j in range(1, MAXGAP + 1):
                lj = c[j] * inv
                low[j, at, :] = lj
                for h in range(MAXGAP - j + 1):
                    term = lj * c[j + h]
                    old = acc.get((j, h))
                    fresh[(j - 1, h)] = term if old is None else old + term
            acc = fresh
        return tuple(acc[k] for k in keys)

    lax.fori_loop(0, PAD // 8, factor_block, tuple(zero for _ in keys))

    member = lax.broadcasted_iota(jnp.int32, (LANES, pixels), 0)
    onehot = jnp.where(member == cls_ref[...], 1.0, 0.0).astype(jnp.bfloat16)

    def expand(value):
        parts = split3(value)
        return dot_nn(parts[0], onehot) + (dot_nn(parts[1], onehot) + dot_nn(parts[2], onehot))

    for g in range(MAXGAP + 1):
        lpx_ref[g] = expand(low[g])
    wpx_ref[...] = expand(wt_ref[...])


def solve_kernel(recv_ref, inc_ref, wpx_ref, lpx_ref, self_ref, left_ref, right_ref, sel_ref,
                 tile_ref, out_ref, rows, x_ref, edge, halo_left, halo_right, halo_tile,
                 send_sem, recv_sem):
    me = lax.axis_index("ifg")
    core = lax.axis_index("tile")
    count = lax.axis_size("ifg")
    left = lax.rem(me + count - 1, count)
    right = lax.rem(me + 1, count)
    other = 1 - core
    partners = [(left, core), (right, core), (me, other), (left, other), (right, other)]
    barrier = pltpu.get_barrier_semaphore()
    for partner in partners:
        pl.semaphore_signal(barrier, inc=1, device_id=partner, device_id_type=MESH)
    pl.semaphore_wait(barrier, len(partners))

    parts = split3(recv_ref[...] * wpx_ref[...])
    inc = inc_ref[...]
    pixels = x_ref.shape[1]
    rows[0:PAD, :] = dot_nn(inc, parts[0]) + (dot_nn(inc, parts[1]) + dot_nn(inc, parts[2]))
    rows[PAD:PAD + 8, :] = jnp.zeros((8, pixels), jnp.float32)

    def forward(block, carry):
        a = list(carry)
        base = pl.multiple_of(block * 8, 8)
        for s in range(8):
            at = pl.ds(base + s, 1)
            y = a[0]
            a = a[1:] + [rows[pl.ds(base + s + 8, 1), :]]
            a = [a[j] - lpx_ref[j + 1, at, :] * y for j in range(8)]
            x_ref[at, :] = y * lpx_ref[0, at, :]
        return tuple(a)

    lax.fori_loop(0, PAD // 8, forward, tuple(rows[d:d + 1, :] for d in range(8)))

    def backward(block, carry):
        later = list(carry)
        base = pl.multiple_of(PAD - 8 - block * 8, 8)
        for s in range(7, -1, -1):
            at = pl.ds(base + s, 1)
            value = x_ref[at, :]
            for g in range(8, 0, -1):
                value = value - lpx_ref[g, at, :] * later[g - 1]
            x_ref[at, :] = value
            later = [value] + later[:7]
        return tuple(later)

    lax.fori_loop(0, PAD // 8, backward, tuple(jnp.zeros((1, pixels), jnp.float32) for _ in range(8)))

    def copy(i, src, dst, device):
        return pltpu.make_async_remote_copy(src_ref=src, dst_ref=dst, send_sem=send_sem.at[i],
                                            recv_sem=recv_sem.at[i], device_id=device,
                                            device_id_type=MESH)

    copies = [copy(0, x_ref, halo_right, (left, core)), copy(1, x_ref, halo_left, (right, core))]
    for c in copies:
        c.start()
    x = x_ref[...]
    edge[...] = dot_nt(sel_ref[...], x, precision=HIGHEST)
    small = [copy(2, edge, halo_tile.at[1], (me, other)),
             copy(3, edge, halo_tile.at[2], (left, other)),
             copy(4, edge, halo_tile.at[0], (right, other))]
    for c in small:
        c.start()
    total = dot_nt(self_ref[...], x, precision=HIGHEST)
    for c in small:
        c.wait()
    for i in range(3):
        total += dot_nn(tile_ref[i], halo_tile[i], precision=HIGHEST)
    copies[0].wait()
    total += dot_nt(right_ref[...], halo_right[...], precision=HIGHEST)
    copies[1].wait()
    total += dot_nt(left_ref[...], halo_left[...], precision=HIGHEST)
    out_ref[...] = total[:, 0:DATES]


def filter_taps():
    offsets = jnp.arange(-R, R + 1).astype(jnp.float32)
    return jnp.sum(jnp.exp(-offsets * offsets / 4.5))


def tap(delta, norm):
    near = jnp.exp(-(delta * delta).astype(jnp.float32) / 4.5) / norm
    return jnp.where(jnp.abs(delta) <= R, near, 0.0)


def filter_matrices(tile_rows, tile_cols):
    norm = filter_taps()
    pixels = tile_rows * tile_cols
    me, core = lax.axis_index("ifg"), lax.axis_index("tile")
    count = lax.axis_size("ifg")
    out = jnp.arange(pixels, dtype=jnp.int32)[:, None]
    out_r, out_c = out // tile_cols, out % tile_cols
    inn = jnp.arange(pixels, dtype=jnp.int32)[None, :]
    in_c, in_r = inn // tile_rows, inn % tile_rows
    vertical = tap(out_r - in_r, norm)
    has_left = jnp.where(me > 0, 1.0, 0.0)
    has_right = jnp.where(me < count - 1, 1.0, 0.0)
    same = jnp.where((out_r == in_r) & (out_c == in_c), 1.0, 0.0)
    own = same - vertical * tap(out_c - in_c, norm)
    left = -has_left * vertical * tap(out_c - in_c + tile_cols, norm)
    right = -has_right * vertical * tap(out_c - in_c - tile_cols, norm)
    slot = jnp.arange(16, dtype=jnp.int32)
    slot_c, slot_j = slot // 4, slot % 4
    sent_r = jnp.where(core == 0, tile_rows - R + slot_j, slot_j)
    sel = jnp.where((slot_j[:, None] < R) & (sent_r[:, None] == in_r) & (slot_c[:, None] == in_c), 1.0, 0.0)
    got_r = jnp.where(core == 0, tile_rows + slot_j, slot_j - R)[None, :]
    reach = jnp.where(slot_j[None, :] < R, tap(out_r - got_r, norm), 0.0)
    tiles = jnp.stack([
        -has * reach * tap(out_c - slot_c[None, :] + shift, norm)
        for has, shift in ((has_left, tile_cols), (1.0, 0), (has_right, -tile_cols))
    ])
    return own, left, right, sel, tiles


def on_device(phases, pairs, class_weights, classes):
    own_ifg, tile_rows, cols = phases.shape
    tile_cols = classes.shape[1]
    pixels = tile_rows * tile_cols
    count = cols // tile_cols
    nifg = pairs.shape[0]
    vmem = pl.BlockSpec(memory_space=pltpu.VMEM)

    blocks = phases.transpose(0, 2, 1).reshape(own_ifg, count, pixels).transpose(1, 0, 2)
    received = lax.all_to_all(blocks, "ifg", split_axis=0, concat_axis=0, tiled=True)
    received = received.reshape(nifg, pixels)

    padded = jnp.pad(class_weights, ((0, LANES - CLASSES), (0, 0)))
    inc, wpx, lpx = pl.pallas_call(
        factor_kernel,
        out_shape=(
            jax.ShapeDtypeStruct((PAD, nifg), jnp.bfloat16),
            jax.ShapeDtypeStruct((nifg, pixels), jnp.float32),
            jax.ShapeDtypeStruct((MAXGAP + 1, PAD, pixels), jnp.float32),
        ),
        in_specs=[vmem] * 4,
        out_specs=(vmem,) * 3,
        scratch_shapes=[
            pltpu.VMEM((MAXGAP + 1, PAD, LANES), jnp.float32),
            pltpu.VMEM((MAXGAP + 1, PAD, LANES), jnp.float32),
        ],
        compiler_params=pltpu.CompilerParams(vmem_limit_bytes=40 * 1024 * 1024),
        cost_estimate=pl.CostEstimate(flops=40_000_000_000, bytes_accessed=6_000_000, transcendentals=0),
        name="factor",
    )(pairs.T, padded, padded.T, classes.T.reshape(1, pixels))

    own, left, right, sel, tiles = filter_matrices(tile_rows, tile_cols)
    corrected = pl.pallas_call(
        solve_kernel,
        out_shape=jax.ShapeDtypeStruct((pixels, DATES), jnp.float32),
        in_specs=[vmem] * 9,
        out_specs=vmem,
        scratch_shapes=[
            pltpu.VMEM((PAD + 8, pixels), jnp.float32),
            pltpu.VMEM((PAD, pixels), jnp.float32),
            pltpu.VMEM((16, PAD), jnp.float32),
            pltpu.VMEM((PAD, pixels), jnp.float32),
            pltpu.VMEM((PAD, pixels), jnp.float32),
            pltpu.VMEM((3, 16, PAD), jnp.float32),
            pltpu.SemaphoreType.DMA((5,)),
            pltpu.SemaphoreType.DMA((5,)),
        ],
        compiler_params=pltpu.CompilerParams(
            collective_id=0, has_side_effects=True, vmem_limit_bytes=40 * 1024 * 1024
        ),
        name="solve",
    )(received, inc, wpx, lpx, own, left, right, sel, tiles)
    return corrected.reshape(tile_rows, tile_cols, DATES)


def solution(mesh):
    return jax.shard_map(
        on_device,
        mesh=mesh,
        in_specs=(P("ifg", "tile", None), P(), P(), P("tile", "ifg")),
        out_specs=P("tile", "ifg", None),
        check_vma=False,
    )
```

time: 470 us -> 68.8 us (0.15); the launches traced: 463 us -> 68 us
  other arithmetic: 336 us -> 2.68 us
  Pallas kernels: 0 us -> 40.5 us
  matrix products: 34.2 us -> 0 us
  waiting for transfers between devices: 37.7 us -> 5.99 us
  between operations: 14.3 us -> 0.16 us
  local copies, waits for them, and re-layouts: 23.4 us -> 11.1 us
  starting transfers between devices: 17.7 us -> 7.55 us
    another operation x23 -> x1, other arithmetic: 315 us -> 0.01 us  [filter_matrices(): jnp.stack([-has * reach * tap(out_c - slot_c[None, :] + shift, norm) for...]
    pallas_call x0 -> x2, Pallas kernels: none -> 40.5 us  [the longest x1 30.3 us: on_device(): pl.pallas_call(solve_kernel, out_shape=jax.ShapeDtypeStruct((pixels, DATE...]
    another operation x14 -> x0, matrix products: 19.2 us -> none  [the longest x10 14.5 us: invert(): jax.scipy.linalg.cho_solve((factor, True), jnp.eye(DATES, dtype=jnp.float...]
    all_to_all x1, waiting for transfers between devices: 22 us -> 5.99 us  [on_device(): lax.all_to_all(blocks, 'ifg', split_axis=0, concat_axis=0, tiled=True)]
    ppermute x4 -> x0, waiting for transfers between devices: 15.7 us -> none  [the longest x2 13.4 us: with_halo(): lax.ppermute(head, axis, [((i + 1) % count, i) for i in range(ends)])]
    dot_general x13 -> x0, matrix products: 15 us -> none  [the longest x8 9.61 us: on_device(): jnp.einsum('pd,ed->pe', right_terms, inverse[member], precision=lax.Preci...]
    ppermute x4 -> x0, starting transfers between devices: 10.1 us -> none  [the longest x2 6.92 us: with_halo(): lax.ppermute(head, axis, [((i + 1) % count, i) for i in range(ends)])]
    another operation x18 -> x1, local copies, waits for them, and re-layouts: 7.16 us -> 0.16 us  [filter_matrices(): jnp.stack([-has * reach * tap(out_c - slot_c[None, :] + shift, norm) for...]
  transfers between devices with their start and end apart: 6 -> 1, of which waited for: 4 -> 1; matrix products, arithmetic and copies ran while one was open for 4% -> 5% of each run, Pallas kernels for 0% -> 15%
where the time goes in v1:
time: 68.8 us; the launch traced here: 68 us
  Pallas kernels  40.5 us (59%)
  local copies, waits for them, and re-layouts  11.1 us (16%)
  starting transfers between devices  7.55 us (11%)
  waiting for transfers between devices  5.99 us (9%)
  other arithmetic  2.68 us (4%)
    pallas_call x1, Pallas kernels, on_device(): pl.pallas_call(solve_kernel, out_shape=jax.ShapeDtypeStruct((pixels, DATE...  30.3 us
    pallas_call x1, Pallas kernels, on_device(): pl.pallas_call(factor_kernel, out_shape=(jax.ShapeDtypeStruct((PAD, nifg)...  10.2 us
    all_to_all x1, starting transfers between devices, on_device(): lax.all_to_all(blocks, 'ifg', split_axis=0, concat_axis=0, tiled=True)  7.55 us
    all_to_all x1, waiting for transfers between devices, on_device(): lax.all_to_all(blocks, 'ifg', split_axis=0, concat_axis=0, tiled=True)  5.99 us
    unnamed x16, local copies, waits for them, and re-layouts  5.91 us
    transpose x2, local copies, waits for them, and re-layouts, on_device(): phases.transpose(0, 2, 1).reshape(own_ifg, count, pixels).transpose(1, 0, 2)  3.5 us
  transfers between devices with their start and end apart: 1, of which 1 were waited for; matrix products, arithmetic and copies ran while one was open for 5% of the time, Pallas kernels for 15%

profile of v1, /device:TPU:1, one launch (start us, length us, event | category | flops | bytes accessed | tf_op | source)
XLA Modules:
  0.0 68.0 jit_solution(72984749966293002)
XLA Ops:
  0.0 1.9 %copy.11 = f32[64,64,64]{2,1,0:T(8,128)S(1)} copy(f32[64,64,64]{1,2,0:T(8,128)} %bitcast.10) | data formatting | bytes 2097152 | tf_op jit(solution)/shard_map/transpose | solution.py:230
  1.9 0.5 reshape.617
  2.5 0.0 copy-start.5
  2.5 1.6 %copy.12 = f32[16,64,256]{2,1,0:T(8,128)} copy(f32[16,64,256]{2,0,1:T(8,128)S(1)} %bitcast.9) | data formatting | bytes 2097152 | tf_op jit(solution)/shard_map/transpose | solution.py:230
  4.1 0.0 copy-start.6
  4.1 0.0 copy-start.4
  4.1 7.5 %all-to-all-start = ((f32[16,64,256]{2,1,0:T(8,128)}), f32[16,64,256]{2,1,0:T(8,128)S(1)}, u32[]{:S(2)}, u32[]{:S(2)}) async-start(f32[16,64,256]{2,1,0:T(8,128)} %copy.12), calls=%async_computation | async-start | bytes 2097152 | tf_op jit(solution)/shard_map/all_to_all | solution.py:231
  11.6 0.0 copy-done.5
  11.6 0.2 copy.13
  11.8 0.2 copy.16
  12.1 0.0 copy-done.6
  12.1 0.1 reshape.619.cls_ref
  12.2 0.0 copy-done.4
  12.2 10.2 %factor.1 = (bf16[304,1024]{1,0:T(8,128)(2,1)S(1)}, f32[1024,256]{1,0:T(8,128)S(1)}, f32[9,304,256]{2,1,0:T(8,128)S(1)}) custom-call(s32[2,1024]{1,0:T(2,128)S(1)} %bitcast.8, f32[128,1024]{1,0:T(8,128)S(1)} %pad.4.clone.w_ref, f32[1024,128]{1,0:T(8,128)S(1)} %pad_bitcast_fusion.wt_ref, s32[1,256]{1,0:T(1,128)S(1)} %reshape.619.cls_ref), custom_call_target="tpu_custom_call" | custom-call | flops 40000000000 | bytes 6000000 | tf_op jit(solution)/shard_map/factor/pallas_call | solution.py:235
  22.4 0.0 copy-start
  22.4 1.5 %copy-done = f32[9,304,256]{2,1,0:T(8,128)} copy-done((f32[9,304,256]{2,1,0:T(8,128)}, f32[9,304,256]{2,1,0:T(8,128)S(1)}, u32[]{:S(2)}) %copy-start) | copy-done | bytes 2801688
  24.0 0.0 copy-start.2
  24.0 1.0 %copy-done.2 = f32[1024,256]{1,0:T(8,128)} copy-done((f32[1024,256]{1,0:T(8,128)}, f32[1024,256]{1,0:T(8,128)S(1)}, u32[]{:S(2)}) %copy-start.2) | copy-done | bytes 1048600
  24.9 0.6 fusion.78
  25.6 0.8 %fusion.55 = (f32[1,256,16]{1,2,0:T(8,128)S(1)}, f32[1,256,16]{1,2,0:T(8,128)S(1)}, f32[1,256,16]{1,2,0:T(8,128)S(1)}) fusion(s32[16]{0:T(128)S(1)} %get-tuple-element.21, s32[256]{0:T(256)S(1)} %get-tuple-element.19, f32[]{:T(128)} %fusion.78, f32[]{:T(128)S(6)} %neg.74, s32[16]{0:T(128)S(1)} %broadcast_select_fusion, s32[256]{0:T(256)S(1)} %get-tuple-element.20, ...), kind=kLoop, calls=%fused_computation.68 | loop fusion | flops 176128 | bytes 51356 | tf_op jit(solution)/shard_map/mul | solution.py:216
  26.4 0.2 copy.15.tile_ref
  26.5 0.1 and_select_fusion.sel_ref
  26.6 1.2 %fusion.11 = (f32[256,256]{1,0:T(8,128)S(1)}, f32[256,256]{1,0:T(8,128)S(1)}, f32[256,256]{1,0:T(8,128)S(1)}) fusion(f32[]{:T(128)S(6)} %neg.76, f32[]{:T(128)} %fusion.78, s32[256]{0:T(256)S(1)} %get-tuple-element.17, s32[256]{0:T(256)S(1)} %get-tuple-element.19, s32[256]{0:T(256)S(1)} %get-tuple-element.18, s32[256]{0:T(256)S(1)} %get-tuple-element.20, ...), kind=kLoop, calls=%fused_computation.17 | loop fusion | flops 3014656 | bytes 790540 | tf_op jit(solution)/shard_map/mul | solution.py:208
  27.8 6.0 %all-to-all-done = f32[16,64,256]{2,1,0:T(8,128)S(1)} async-done(((f32[16,64,256]{2,1,0:T(8,128)}), f32[16,64,256]{2,1,0:T(8,128)S(1)}, u32[]{:S(2)}, u32[]{:S(2)}) %all-to-all-start) | async-done | bytes 1048608 | tf_op jit(solution)/shard_map/all_to_all | solution.py:231
  33.8 0.0 copy-start.1
  33.8 1.8 %copy-done.1 = f32[9,304,256]{2,1,0:T(8,128)S(1)} copy-done((f32[9,304,256]{2,1,0:T(8,128)S(1)}, f32[9,304,256]{2,1,0:T(8,128)}, u32[]{:S(2)}) %copy-start.1) | copy-done | bytes 2801688
  35.6 0.0 copy-start.3
  35.6 1.2 %copy-done.3 = f32[1024,256]{1,0:T(8,128)S(1)} copy-done((f32[1024,256]{1,0:T(8,128)S(1)}, f32[1024,256]{1,0:T(8,128)}, u32[]{:S(2)}) %copy-start.3) | copy-done | bytes 1048600
  36.8 30.3 %solve.1 = f32[256,300]{1,0:T(8,128)S(1)} custom-call(f32[1024,256]{1,0:T(8,128)S(1)} %bitcast.7, bf16[304,1024]{1,0:T(8,128)(2,1)S(1)} %get-tuple-element.8.inc_ref, f32[1024,256]{1,0:T(8,128)S(1)} %copy-done.3, f32[9,304,256]{2,1,0:T(8,128)S(1)} %copy-done.1, f32[256,256]{1,0:T(8,128)S(1)} %get-tuple-element.13.self_ref, ...), custom_call_target="tpu_custom_call" | custom-call | tf_op jit(solution)/shard_map/solve/pallas_call | solution.py:254
  67.2 0.9 %reshape.620 = f32[64,4,300]{2,1,0:T(4,128)} reshape(f32[256,300]{1,0:T(8,128)S(1)} %solve.1) | data formatting | bytes 614400 | tf_op jit(solution)/shard_map/reshape | solution.py:274
  (8 shorter events, 0.1 us)
Async XLA Ops:
  2.5 9.2 %copy-start.5 = (f32[8,1024]{1,0:T(8,128)S(1)}, f32[8,1024]{1,0:T(8,128)}, u32[]{:S(2)}) copy-start(f32[8,1024]{1,0:T(8,128)} %param.6) | copy-start | bytes 98308
  4.1 8.0 %copy-start.6 = (s32[64,4]{0,1:T(4,128)S(1)}, s32[64,4]{0,1:T(4,128)}, u32[]{:S(2)}) copy-start(s32[64,4]{0,1:T(4,128)} %param.7) | copy-start | bytes 3076
  4.1 8.1 %copy-start.4 = (s32[1024,2]{0,1:T(2,128)S(1)}, s32[1024,2]{0,1:T(2,128)}, u32[]{:S(2)}) copy-start(s32[1024,2]{0,1:T(2,128)} %param.5) | copy-start | bytes 24580
  4.1 29.7 %all-to-all-start = ((f32[16,64,256]{2,1,0:T(8,128)}), f32[16,64,256]{2,1,0:T(8,128)S(1)}, u32[]{:S(2)}, u32[]{:S(2)}) async-start(f32[16,64,256]{2,1,0:T(8,128)} %copy.12), calls=%async_computation | async-start | bytes 2097152 | tf_op jit(solution)/shard_map/all_to_all | solution.py:231
  22.4 1.6 %copy-start = (f32[9,304,256]{2,1,0:T(8,128)}, f32[9,304,256]{2,1,0:T(8,128)S(1)}, u32[]{:S(2)}) copy-start(f32[9,304,256]{2,1,0:T(8,128)S(1)} %get-tuple-element.10.lpx_ref) | copy-start | bytes 8404996
  24.0 1.0 %copy-start.2 = (f32[1024,256]{1,0:T(8,128)}, f32[1024,256]{1,0:T(8,128)S(1)}, u32[]{:S(2)}) copy-start(f32[1024,256]{1,0:T(8,128)S(1)} %get-tuple-element.9.wpx_ref) | copy-start | bytes 3145732
  33.8 1.8 %copy-start.1 = (f32[9,304,256]{2,1,0:T(8,128)S(1)}, f32[9,304,256]{2,1,0:T(8,128)}, u32[]{:S(2)}) copy-start(f32[9,304,256]{2,1,0:T(8,128)} %copy-done) | copy-start | bytes 8404996
  35.6 1.2 %copy-start.3 = (f32[1024,256]{1,0:T(8,128)S(1)}, f32[1024,256]{1,0:T(8,128)}, u32[]{:S(2)}) copy-start(f32[1024,256]{1,0:T(8,128)} %copy-done.2) | copy-start | bytes 3145732

commit v2 on v1

v2 whole, which is shorter than its diff:
```python
import functools
import math
import jax
import jax.numpy as jnp
from jax import lax
from jax.experimental import pallas as pl
from jax.experimental.pallas import tpu as pltpu
from jax.sharding import PartitionSpec as P

DATES = 300
CLASSES = 8
MAXGAP = 8
R = 3
LANES = 128
PAD = -(-DATES // 8) * 8
CHUNKS = 4
MESH = pl.DeviceIdType.MESH
HIGHEST = lax.Precision.HIGHEST

smooth_weight = 1.0
anchor_weight = 0.1


def split3(value):
    high = value.astype(jnp.bfloat16)
    rest = value - high.astype(jnp.float32)
    middle = rest.astype(jnp.bfloat16)
    low = (rest - middle.astype(jnp.float32)).astype(jnp.bfloat16)
    return (high, middle, low)


def dot_nt(a, b, **kw):
    return lax.dot_general(a, b, (((1,), (1,)), ((), ())), preferred_element_type=jnp.float32, **kw)


def dot_nn(a, b, **kw):
    return lax.dot_general(a, b, (((1,), (0,)), ((), ())), preferred_element_type=jnp.float32, **kw)


def factor(pairs_ref, w_ref, wt_ref, cls_ref, inc_ref, wpx_ref, lpx_ref, band, low):
    nifg = pairs_ref.shape[1]
    pixels = cls_ref.shape[1]
    first = pairs_ref[0:1, :]
    second = pairs_ref[1:2, :]
    gap = second - first
    dates = lax.broadcasted_iota(jnp.int32, (PAD, nifg), 0)
    minus_f = jnp.where(dates == first, 1.0, 0.0)
    plus_f = jnp.where(dates == second, 1.0, 0.0)
    inc_ref[...] = (plus_f - minus_f).astype(jnp.bfloat16)
    minus = minus_f.astype(jnp.bfloat16)
    both = (plus_f + minus_f).astype(jnp.bfloat16)
    w = w_ref[...]
    row = lax.broadcasted_iota(jnp.int32, (PAD, LANES), 0)
    inside = lambda ok: jnp.where(ok, 1.0, 0.0)
    for g in range(MAXGAP + 1):
        parts = split3(w if g == 0 else jnp.where(gap == g, w, 0.0))
        left = both if g == 0 else minus
        total = dot_nt(left, parts[0]) + (dot_nt(left, parts[1]) + dot_nt(left, parts[2]))
        here = inside(row <= DATES - 3)
        before = inside((row >= 1) & (row <= DATES - 2))
        if g == 0:
            twice = inside((row >= 2) & (row <= DATES - 1))
            prior = smooth_weight * (here + 4.0 * before + twice) + anchor_weight
            total = total + jnp.where(row < DATES, prior, 1.0)
        elif g == 1:
            total = smooth_weight * (-2.0 * here - 2.0 * before) - total
        elif g == 2:
            total = smooth_weight * here - total
        else:
            total = -total
        band[g] = total

    zero = jnp.zeros((1, LANES), jnp.float32)
    keys = [(j, h) for j in range(MAXGAP) for h in range(MAXGAP - j)]

    def factor_block(block, carry):
        acc = dict(zip(keys, carry))
        base = pl.multiple_of(block * 8, 8)
        for s in range(8):
            at = pl.ds(base + s, 1)
            c = [band[h, at, :] for h in range(MAXGAP + 1)]
            c = [c[h] - acc[(0, h)] for h in range(MAXGAP)] + [c[MAXGAP]]
            inv = 1.0 / c[0]
            low[0, at, :] = inv
            fresh = {}
            for j in range(1, MAXGAP + 1):
                lj = c[j] * inv
                low[j, at, :] = lj
                for h in range(MAXGAP - j + 1):
                    term = lj * c[j + h]
                    old = acc.get((j, h))
                    fresh[(j - 1, h)] = term if old is None else old + term
            acc = fresh
        return tuple(acc[k] for k in keys)

    lax.fori_loop(0, PAD // 8, factor_block, tuple(zero for _ in keys))

    member = lax.broadcasted_iota(jnp.int32, (LANES, pixels), 0)
    onehot = jnp.where(member == cls_ref[...], 1.0, 0.0).astype(jnp.bfloat16)

    def expand(value):
        parts = split3(value)
        return dot_nn(parts[0], onehot) + (dot_nn(parts[1], onehot) + dot_nn(parts[2], onehot))

    for g in range(MAXGAP + 1):
        lpx_ref[g] = expand(low[g])
    wpx_ref[...] = expand(wt_ref[...])


NORM = sum(math.exp(-j * j / 4.5) for j in range(-R, R + 1))


def tap(delta):
    near = jnp.exp((delta * delta).astype(jnp.float32) * (-1.0 / 4.5)) * (1.0 / NORM)
    return jnp.where(jnp.abs(delta) <= R, near, 0.0)


def split_index(index, size):
    if size & (size - 1):
        return index // size, index % size
    return index >> (size.bit_length() - 1), index & (size - 1)


def iota(shape, dim):
    return lax.broadcasted_iota(jnp.int32, shape, dim)


def fill_filters(tile_rows, tile_cols, own_ref, left_ref, right_ref, sel_ref, tile_ref):
    pixels = tile_rows * tile_cols
    me, core = lax.axis_index("ifg"), lax.axis_index("tile")
    count = lax.axis_size("ifg")
    has_left = jnp.where(me > 0, 1.0, 0.0)
    has_right = jnp.where(me < count - 1, 1.0, 0.0)
    square = (pixels, pixels)
    out_r, out_c = split_index(iota(square, 0), tile_cols)
    in_c, in_r = split_index(iota(square, 1), tile_rows)
    vertical = tap(out_r - in_r)
    same = jnp.where((out_r == in_r) & (out_c == in_c), 1.0, 0.0)
    own_ref[...] = same - vertical * tap(out_c - in_c)
    from_left = jnp.where(in_c >= 2, 1, in_c + 2)
    from_right = jnp.where(in_c >= 2, 2, in_c)
    left = -has_left * vertical * tap(out_c - from_left + tile_cols)
    right = -has_right * vertical * tap(out_c - from_right - tile_cols)
    for ref, value in ((left_ref, left), (right_ref, right)):
        parts = split3(value)
        ref[0] = parts[0]
        ref[1] = parts[1]
    slot_c, slot_j = split_index(iota((16, pixels), 0), 4)
    sel_c, sel_r = split_index(iota((16, pixels), 1), tile_rows)
    sent_r = jnp.where(core == 0, tile_rows - R, 0) + slot_j
    sel_ref[...] = jnp.where((slot_j < R) & (sent_r == sel_r) & (slot_c == sel_c), 1.0, 0.0)
    slot_c, slot_j = split_index(iota((pixels, 16), 1), 4)
    out_r, out_c = split_index(iota((pixels, 16), 0), tile_cols)
    got_r = jnp.where(core == 0, tile_rows, -R) + slot_j
    reach = jnp.where(slot_j < R, tap(out_r - got_r), 0.0)
    tile_ref[0] = -has_left * reach * tap(out_c - slot_c + tile_cols)
    tile_ref[1] = -reach * tap(out_c - slot_c)
    tile_ref[2] = -has_right * reach * tap(out_c - slot_c - tile_cols)


def kernel(tile_rows, tile_cols, blocks_ref, pairs_ref, w_ref, wt_ref, cls_ref, out_ref,
           recv, inc_ref, wpx_ref, lpx_ref, band, low, own_ref, left_ref, right_ref, sel_ref,
           tile_ref, rows, x_ref, spare, edge, halo_pair, halo_spare, halo_tile,
           all_send, all_recv, own_sem, send_sem, recv_sem):
    me = lax.axis_index("ifg")
    core = lax.axis_index("tile")
    count = lax.axis_size("ifg")
    left = lax.rem(me + count - 1, count)
    right = lax.rem(me + 1, count)
    other = 1 - core
    near = [(me, other), (left, other), (right, other)]
    barrier = pltpu.get_barrier_semaphore()

    def greet(k, _):
        pl.semaphore_signal(barrier, inc=1, device_id=(lax.rem(me + k, count), core), device_id_type=MESH)
        return _

    lax.fori_loop(1, count, greet, 0)
    for partner in near:
        pl.semaphore_signal(barrier, inc=1, device_id=partner, device_id_type=MESH)
    pl.semaphore_wait(barrier, count - 1 + len(near))

    def exchange(k, slot):
        peer = lax.rem(me + k, count)
        return pltpu.make_async_remote_copy(
            src_ref=blocks_ref.at[peer], dst_ref=recv.at[slot], send_sem=all_send.at[k],
            recv_sem=all_recv.at[k], device_id=(peer, core), device_id_type=MESH)

    def send_block(k, _):
        exchange(k, me).start()
        return _

    lax.fori_loop(1, count, send_block, 0)
    mine = pltpu.make_async_copy(blocks_ref.at[me], recv.at[me], own_sem)
    mine.start()

    factor(pairs_ref, w_ref, wt_ref, cls_ref, inc_ref, wpx_ref, lpx_ref, band, low)
    fill_filters(tile_rows, tile_cols, own_ref, left_ref, right_ref, sel_ref, tile_ref)

    def take_block(k, _):
        exchange(k, lax.rem(me + count - k, count)).wait()
        return _

    mine.wait()
    lax.fori_loop(1, count, take_block, 0)

    pixels = x_ref.shape[1]
    parts = split3(recv[...].reshape(-1, pixels) * wpx_ref[...])
    inc = inc_ref[...]
    rows[0:PAD, :] = dot_nn(inc, parts[0]) + dot_nn(inc, parts[1])
    rows[PAD:PAD + 8, :] = jnp.zeros((8, pixels), jnp.float32)

    def forward(block, carry):
        a = list(carry)
        base = pl.multiple_of(block * 8, 8)
        for s in range(8):
            at = pl.ds(base + s, 1)
            y = a[0]
            a = a[1:] + [rows[pl.ds(base + s + 8, 1), :]]
            a = [a[j] - lpx_ref[j + 1, at, :] * y for j in range(8)]
            x_ref[at, :] = y * lpx_ref[0, at, :]
        return tuple(a)

    lax.fori_loop(0, PAD // 8, forward, tuple(rows[d:d + 1, :] for d in range(8)))

    def backward(block, carry):
        later = list(carry)
        base = pl.multiple_of(block * 8, 8)
        for s in range(7, -1, -1):
            at = pl.ds(base + s, 1)
            value = x_ref[at, :]
            for g in range(8, 0, -1):
                value = value - lpx_ref[g, at, :] * later[g - 1]
            x_ref[at, :] = value
            later = [value] + later[:7]
        return tuple(later)

    def copy(i, src, dst, device):
        return pltpu.make_async_remote_copy(src_ref=src, dst_ref=dst, send_sem=send_sem.at[i],
                                            recv_sem=recv_sem.at[i], device_id=device,
                                            device_id_type=MESH)

    half = pixels // 2
    total_blocks = PAD // 8
    cuts = [total_blocks * (CHUNKS - i) // CHUNKS for i in range(CHUNKS + 1)]
    carry = tuple(jnp.zeros((1, pixels), jnp.float32) for _ in range(8))
    to_left, to_right = [], []
    for i in range(CHUNKS):
        top, bottom = cuts[i], cuts[i + 1]
        carry = lax.fori_loop(0, top - bottom, lambda n, c, top=top: backward(top - 1 - n, c), carry)
        span = pl.ds(bottom * 8, (top - bottom) * 8)
        to_left.append(copy(2 * i, x_ref.at[span, pl.ds(0, half)], halo_pair.at[1, span], (left, core)))
        to_right.append(copy(2 * i + 1, x_ref.at[span, pl.ds(half, half)], halo_pair.at[0, span], (right, core)))
        to_left[-1].start()
        to_right[-1].start()
    x = x_ref[...]
    mid = PAD // 2
    low_lanes = iota((mid, half), 1) < half // 2
    first, second = x[:, 0:half], x[:, half:]
    spare[0] = jnp.where(low_lanes, pltpu.roll(first[0:mid], half // 2, 1), first[mid:])
    spare[1] = jnp.where(low_lanes, second[0:mid], pltpu.roll(second[mid:], half // 2, 1))
    to_right.append(copy(2 * CHUNKS, spare.at[0], halo_spare.at[0], (right, core)))
    to_left.append(copy(2 * CHUNKS + 1, spare.at[1], halo_spare.at[1], (left, core)))
    to_right[-1].start()
    to_left[-1].start()
    edge[...] = dot_nt(sel_ref[...], x, precision=HIGHEST)
    small = [copy(2 * CHUNKS + 2 + i, edge, halo_tile.at[slot], near[i]) for i, slot in enumerate((1, 2, 0))]
    for c in small:
        c.start()
    total = dot_nt(own_ref[...], x, precision=HIGHEST)
    for c in small:
        c.wait()
    for i in range(3):
        total += dot_nn(tile_ref[i], halo_tile[i], precision=HIGHEST)
    for c in to_right + to_left:
        c.wait()
    keep = (iota((PAD, half), 0) < mid) == (iota((PAD, half), 1) < half // 2)
    for side, ref in ((0, left_ref), (1, right_ref)):
        again = halo_spare[side]
        extra = jnp.where(keep, jnp.concatenate([again, again], axis=0), 0.0)
        high, middle, _ = split3(jnp.concatenate([halo_pair[side], extra], axis=1))
        total = total + (dot_nt(ref[0], high) + (dot_nt(ref[0], middle) + dot_nt(ref[1], high)))
    out_ref[...] = total[:, 0:DATES]


def on_device(phases, pairs, class_weights, classes):
    own_ifg, tile_rows, cols = phases.shape
    tile_cols = classes.shape[1]
    pixels = tile_rows * tile_cols
    count = cols // tile_cols
    nifg = pairs.shape[0]
    half = pixels // 2
    vmem = pl.BlockSpec(memory_space=pltpu.VMEM)
    f32, bf16 = jnp.float32, jnp.bfloat16
    copies = 2 * CHUNKS + 5

    blocks = phases.transpose(0, 2, 1).reshape(own_ifg, count, pixels).transpose(1, 0, 2)
    padded = jnp.pad(class_weights, ((0, LANES - CLASSES), (0, 0)))
    corrected = pl.pallas_call(
        functools.partial(kernel, tile_rows, tile_cols),
        out_shape=jax.ShapeDtypeStruct((pixels, DATES), f32),
        in_specs=[vmem] * 5,
        out_specs=vmem,
        scratch_shapes=[
            pltpu.VMEM((count, own_ifg, pixels), f32),
            pltpu.VMEM((PAD, nifg), bf16),
            pltpu.VMEM((nifg, pixels), f32),
            pltpu.VMEM((MAXGAP + 1, PAD, pixels), f32),
            pltpu.VMEM((MAXGAP + 1, PAD, LANES), f32),
            pltpu.VMEM((MAXGAP + 1, PAD, LANES), f32),
            pltpu.VMEM((pixels, pixels), f32),
            pltpu.VMEM((2, pixels, pixels), bf16),
            pltpu.VMEM((2, pixels, pixels), bf16),
            pltpu.VMEM((16, pixels), f32),
            pltpu.VMEM((3, pixels, 16), f32),
            pltpu.VMEM((PAD + 8, pixels), f32),
            pltpu.VMEM((PAD, pixels), f32),
            pltpu.VMEM((2, PAD // 2, half), f32),
            pltpu.VMEM((16, PAD), f32),
            pltpu.VMEM((2, PAD, half), f32),
            pltpu.VMEM((2, PAD // 2, half), f32),
            pltpu.VMEM((3, 16, PAD), f32),
            pltpu.SemaphoreType.DMA((count,)),
            pltpu.SemaphoreType.DMA((count,)),
            pltpu.SemaphoreType.DMA,
            pltpu.SemaphoreType.DMA((copies,)),
            pltpu.SemaphoreType.DMA((copies,)),
        ],
        compiler_params=pltpu.CompilerParams(
            collective_id=0, has_side_effects=True, vmem_limit_bytes=48 * 1024 * 1024
        ),
        name="invert_and_filter",
    )(blocks, pairs.T, padded, padded.T, classes.T.reshape(1, pixels))
    return corrected.reshape(tile_rows, tile_cols, DATES)


def solution(mesh):
    return jax.shard_map(
        on_device,
        mesh=mesh,
        in_specs=(P("ifg", "tile", None), P(), P(), P("tile", "ifg")),
        out_specs=P("tile", "ifg", None),
        check_vma=False,
    )
```

time: 68.8 us -> 51.6 us (0.75)
  starting transfers between devices: 7.55 us -> 0 us
  local copies, waits for them, and re-layouts: 11.1 us -> 4.47 us
  Pallas kernels: 40.5 us -> 46.8 us
  waiting for transfers between devices: 5.99 us -> 0 us
  other arithmetic: 2.68 us -> 0 us
    all_to_all x1 -> x0, starting transfers between devices: 7.55 us -> none  [on_device(): lax.all_to_all(blocks, 'ifg', split_axis=0, concat_axis=0, tiled=True)]
    pallas_call x2 -> x1, Pallas kernels: 40.5 us -> 46.8 us  [on_device(): pl.pallas_call(functools.partial(kernel, tile_rows, tile_cols), out_shape...]
    all_to_all x1 -> x0, waiting for transfers between devices: 5.99 us -> none  [on_device(): lax.all_to_all(blocks, 'ifg', split_axis=0, concat_axis=0, tiled=True)]
    unnamed x16 -> x8, local copies, waits for them, and re-layouts: 5.91 us -> 0.38 us
    mul x2 -> x0, other arithmetic: 1.96 us -> none  [the longest x1 1.21 us: filter_matrices(): right = -has_right * vertical * tap(out_c - in_c - tile_cols, norm)]
    transpose x2 -> x1, local copies, waits for them, and re-layouts: 3.5 us -> 1.92 us  [on_device(): phases.transpose(0, 2, 1).reshape(own_ifg, count, pixels).transpose(1, 0, 2)]
  transfers between devices with their start and end apart: 1 -> 0, of which waited for: 1 -> 0; matrix products, arithmetic and copies ran while one was open for 5% -> 0% of each run, Pallas kernels for 15% -> 0%
where the time goes in v2:
time: 51.6 us; the launch traced here: 51.4 us
  Pallas kernels  46.8 us (91%)
  local copies, waits for them, and re-layouts  4.47 us (9%)
    pallas_call x1, Pallas kernels, on_device(): pl.pallas_call(functools.partial(kernel, tile_rows, tile_cols), out_shape...  46.8 us
    transpose x1, local copies, waits for them, and re-layouts, on_device(): phases.transpose(0, 2, 1).reshape(own_ifg, count, pixels).transpose(1, 0, 2)  1.92 us
    reshape x2, local copies, waits for them, and re-layouts, on_device(): phases.transpose(0, 2, 1).reshape(own_ifg, count, pixels).transpose(1, 0, 2)  1.14 us

profile of v2, /device:TPU:1, one launch (start us, length us, event | category | flops | bytes accessed | tf_op | source)
XLA Modules:
  0.0 51.4 jit_solution(3275215757205819077)
XLA Ops:
  0.0 1.9 %copy.7 = f32[64,64,64]{2,1,0:T(8,128)S(1)} copy(f32[64,64,64]{1,2,0:T(8,128)} %bitcast.10) | data formatting | bytes 2097152 | tf_op jit(solution)/shard_map/transpose | solution.py:297
  1.9 0.0 copy-start.1
  1.9 0.5 %reshape.9 = f32[64,16,256]{2,1,0:T(8,128)S(1)} reshape(f32[64,64,64]{2,1,0:T(8,128)S(1)} %copy.7) | data formatting | bytes 2097152 | tf_op jit(solution)/shard_map/reshape | solution.py:297
  2.5 0.0 copy-start.2
  2.5 0.0 copy-start
  2.5 0.6 %copy.13 = f32[64,16,256]{2,0,1:T(8,128)S(1)} copy(f32[64,16,256]{2,1,0:T(8,128)S(1)} %reshape.9) | data formatting | bytes 2097152 | tf_op jit(solution)/shard_map/reshape | solution.py:297
  3.1 0.0 copy-done.1
  3.1 0.2 copy.9
  3.3 0.2 copy.12
  3.5 0.1 pad.4.clone.w_ref
  3.6 0.0 copy-done.2
  3.6 0.1 reshape.10.cls_ref
  3.7 0.0 copy-done
  3.7 46.8 %invert_and_filter.1 = f32[256,300]{1,0:T(8,128)S(1)} custom-call(f32[16,64,256]{2,1,0:T(8,128)S(1)} %bitcast.8, s32[2,1024]{1,0:T(2,128)S(1)} %bitcast.9, f32[128,1024]{1,0:T(8,128)S(1)} %pad.4.clone.w_ref, f32[1024,128]{1,0:T(8,128)S(1)} %pad_bitcast_fusion.wt_ref, s32[1,256]{1,0:T(1,128)S(1)} %reshape.10.cls_ref), custom_call_target="tpu_custom_call" | custom-call | tf_op jit(solution)/shard_map/invert_and_filter/pallas_call | solution.py:299
  50.6 0.9 %reshape.11 = f32[64,4,300]{2,1,0:T(4,128)} reshape(f32[256,300]{1,0:T(8,128)S(1)} %invert_and_filter.1) | data formatting | bytes 614400 | tf_op jit(solution)/shard_map/reshape | solution.py:334
  (1 shorter events, 0.0 us)
Async XLA Ops:
  1.9 1.2 %copy-start.1 = (f32[8,1024]{1,0:T(8,128)S(1)}, f32[8,1024]{1,0:T(8,128)}, u32[]{:S(2)}) copy-start(f32[8,1024]{1,0:T(8,128)} %param.6) | copy-start | bytes 98308
  2.5 1.1 %copy-start.2 = (s32[64,4]{0,1:T(4,128)S(1)}, s32[64,4]{0,1:T(4,128)}, u32[]{:S(2)}) copy-start(s32[64,4]{0,1:T(4,128)} %param.7) | copy-start | bytes 3076
  2.5 1.2 %copy-start = (s32[1024,2]{0,1:T(2,128)S(1)}, s32[1024,2]{0,1:T(2,128)}, u32[]{:S(2)}) copy-start(s32[1024,2]{0,1:T(2,128)} %param.5) | copy-start | bytes 24580

commit v3 on v2

--- a/solution.py
+++ b/solution.py
@@ -13,7 +13,7 @@
 R = 3
 LANES = 128
 PAD = -(-DATES // 8) * 8
-CHUNKS = 4
+CHUNKS = (2, 4)
 MESH = pl.DeviceIdType.MESH
 HIGHEST = lax.Precision.HIGHEST
 
@@ -103,7 +103,9 @@
         return dot_nn(parts[0], onehot) + (dot_nn(parts[1], onehot) + dot_nn(parts[2], onehot))
 
     for g in range(MAXGAP + 1):
-        lpx_ref[g] = expand(low[g])
+        value = expand(low[g])
+        lpx_ref[0, g] = value[:, 0:pixels // 2]
+        lpx_ref[1, g] = value[:, pixels // 2:]
     wpx_ref[...] = expand(wt_ref[...])
 
 
@@ -180,91 +182,99 @@
         pl.semaphore_signal(barrier, inc=1, device_id=partner, device_id_type=MESH)
     pl.semaphore_wait(barrier, count - 1 + len(near))
 
-    def exchange(k, slot):
+    def exchange(part, k, slot):
         peer = lax.rem(me + k, count)
         return pltpu.make_async_remote_copy(
-            src_ref=blocks_ref.at[peer], dst_ref=recv.at[slot], send_sem=all_send.at[k],
-            recv_sem=all_recv.at[k], device_id=(peer, core), device_id_type=MESH)
-
-    def send_block(k, _):
-        exchange(k, me).start()
-        return _
-
-    lax.fori_loop(1, count, send_block, 0)
-    mine = pltpu.make_async_copy(blocks_ref.at[me], recv.at[me], own_sem)
-    mine.start()
+            src_ref=blocks_ref.at[part, peer], dst_ref=recv.at[part, slot],
+            send_sem=all_send.at[part, k], recv_sem=all_recv.at[part, k],
+            device_id=(peer, core), device_id_type=MESH)
+
+    def own_copy(part):
+        return pltpu.make_async_copy(blocks_ref.at[part, me], recv.at[part, me], own_sem.at[part])
+
+    for part in range(2):
+        def send_block(k, _, part=part):
+            exchange(part, k, me).start()
+            return _
+
+        lax.fori_loop(1, count, send_block, 0)
+        own_copy(part).start()
 
     factor(pairs_ref, w_ref, wt_ref, cls_ref, inc_ref, wpx_ref, lpx_ref, band, low)
-    fill_filters(tile_rows, tile_cols, own_ref, left_ref, right_ref, sel_ref, tile_ref)
-
-    def take_block(k, _):
-        exchange(k, lax.rem(me + count - k, count)).wait()
-        return _
-
-    mine.wait()
-    lax.fori_loop(1, count, take_block, 0)
-
-    pixels = x_ref.shape[1]
-    parts = split3(recv[...].reshape(-1, pixels) * wpx_ref[...])
-    inc = inc_ref[...]
-    rows[0:PAD, :] = dot_nn(inc, parts[0]) + dot_nn(inc, parts[1])
-    rows[PAD:PAD + 8, :] = jnp.zeros((8, pixels), jnp.float32)
-
-    def forward(block, carry):
-        a = list(carry)
-        base = pl.multiple_of(block * 8, 8)
-        for s in range(8):
-            at = pl.ds(base + s, 1)
-            y = a[0]
-            a = a[1:] + [rows[pl.ds(base + s + 8, 1), :]]
-            a = [a[j] - lpx_ref[j + 1, at, :] * y for j in range(8)]
-            x_ref[at, :] = y * lpx_ref[0, at, :]
-        return tuple(a)
-
-    lax.fori_loop(0, PAD // 8, forward, tuple(rows[d:d + 1, :] for d in range(8)))
-
-    def backward(block, carry):
-        later = list(carry)
-        base = pl.multiple_of(block * 8, 8)
-        for s in range(7, -1, -1):
-            at = pl.ds(base + s, 1)
-            value = x_ref[at, :]
-            for g in range(8, 0, -1):
-                value = value - lpx_ref[g, at, :] * later[g - 1]
-            x_ref[at, :] = value
-            later = [value] + later[:7]
-        return tuple(later)
 
     def copy(i, src, dst, device):
         return pltpu.make_async_remote_copy(src_ref=src, dst_ref=dst, send_sem=send_sem.at[i],
                                             recv_sem=recv_sem.at[i], device_id=device,
                                             device_id_type=MESH)
 
-    half = pixels // 2
-    total_blocks = PAD // 8
-    cuts = [total_blocks * (CHUNKS - i) // CHUNKS for i in range(CHUNKS + 1)]
-    carry = tuple(jnp.zeros((1, pixels), jnp.float32) for _ in range(8))
-    to_left, to_right = [], []
-    for i in range(CHUNKS):
-        top, bottom = cuts[i], cuts[i + 1]
-        carry = lax.fori_loop(0, top - bottom, lambda n, c, top=top: backward(top - 1 - n, c), carry)
-        span = pl.ds(bottom * 8, (top - bottom) * 8)
-        to_left.append(copy(2 * i, x_ref.at[span, pl.ds(0, half)], halo_pair.at[1, span], (left, core)))
-        to_right.append(copy(2 * i + 1, x_ref.at[span, pl.ds(half, half)], halo_pair.at[0, span], (right, core)))
-        to_left[-1].start()
-        to_right[-1].start()
-    x = x_ref[...]
+    half = x_ref.shape[2]
     mid = PAD // 2
     low_lanes = iota((mid, half), 1) < half // 2
-    first, second = x[:, 0:half], x[:, half:]
-    spare[0] = jnp.where(low_lanes, pltpu.roll(first[0:mid], half // 2, 1), first[mid:])
-    spare[1] = jnp.where(low_lanes, second[0:mid], pltpu.roll(second[mid:], half // 2, 1))
-    to_right.append(copy(2 * CHUNKS, spare.at[0], halo_spare.at[0], (right, core)))
-    to_left.append(copy(2 * CHUNKS + 1, spare.at[1], halo_spare.at[1], (left, core)))
-    to_right[-1].start()
-    to_left[-1].start()
+    rows[PAD:PAD + 8, :] = jnp.zeros((8, half), jnp.float32)
+    sent = ([], [])
+    at_copy = 0
+    for part in range(2):
+        lanes = pl.ds(part * half, half)
+
+        def take_block(k, _, part=part):
+            exchange(part, k, lax.rem(me + count - k, count)).wait()
+            return _
+
+        own_copy(part).wait()
+        lax.fori_loop(1, count, take_block, 0)
+        high, middle, _ = split3(recv[part].reshape(-1, half) * wpx_ref[:, lanes])
+        both = dot_nn(inc_ref[...], jnp.concatenate([high, middle], axis=1))
+        rows[0:PAD, :] = both[:, 0:half] + both[:, half:]
+
+        def forward(block, carry, part=part):
+            a = list(carry)
+            base = pl.multiple_of(block * 8, 8)
+            for s in range(8):
+                at = pl.ds(base + s, 1)
+                y = a[0]
+                a = a[1:] + [rows[pl.ds(base + s + 8, 1), :]]
+                a = [a[j] - lpx_ref[part, j + 1, at, :] * y for j in range(8)]
+                x_ref[part, at, :] = y * lpx_ref[part, 0, at, :]
+            return tuple(a)
+
+        lax.fori_loop(0, PAD // 8, forward, tuple(rows[d:d + 1, :] for d in range(8)))
+
+        def backward(block, carry, part=part):
+            later = list(carry)
+            base = pl.multiple_of(block * 8, 8)
+            for s in range(7, -1, -1):
+                at = pl.ds(base + s, 1)
+                value = x_ref[part, at, :]
+                for g in range(8, 0, -1):
+                    value = value - lpx_ref[part, g, at, :] * later[g - 1]
+                x_ref[part, at, :] = value
+                later = [value] + later[:7]
+            return tuple(later)
+
+        toward, back = ((left, core), (right, core)) if part == 0 else ((right, core), (left, core))
+        blocks = PAD // 8
+        chunks = CHUNKS[part]
+        cuts = [blocks * (chunks - i) // chunks for i in range(chunks + 1)]
+        carry = tuple(jnp.zeros((1, half), jnp.float32) for _ in range(8))
+        for top, bottom in zip(cuts[:-1], cuts[1:]):
+            carry = lax.fori_loop(0, top - bottom, lambda n, c, top=top, run=backward: run(top - 1 - n, c), carry)
+            span = pl.ds(bottom * 8, (top - bottom) * 8)
+            sent[1 - part].append(copy(at_copy, x_ref.at[part, span], halo_pair.at[1 - part, span], toward))
+            sent[1 - part][-1].start()
+            at_copy += 1
+        piece = x_ref[part]
+        if part == 0:
+            spare[0] = jnp.where(low_lanes, pltpu.roll(piece[0:mid], half // 2, 1), piece[mid:])
+        else:
+            spare[1] = jnp.where(low_lanes, piece[0:mid], pltpu.roll(piece[mid:], half // 2, 1))
+        sent[part].append(copy(at_copy, spare.at[part], halo_spare.at[part], back))
+        sent[part][-1].start()
+        at_copy += 1
+        if part == 0:
+            fill_filters(tile_rows, tile_cols, own_ref, left_ref, right_ref, sel_ref, tile_ref)
+    x = jnp.concatenate([x_ref[0], x_ref[1]], axis=1)
     edge[...] = dot_nt(sel_ref[...], x, precision=HIGHEST)
-    small = [copy(2 * CHUNKS + 2 + i, edge, halo_tile.at[slot], near[i]) for i, slot in enumerate((1, 2, 0))]
+    small = [copy(at_copy + i, edge, halo_tile.at[slot], near[i]) for i, slot in enumerate((1, 2, 0))]
     for c in small:
         c.start()
     total = dot_nt(own_ref[...], x, precision=HIGHEST)
@@ -272,10 +282,10 @@
         c.wait()
     for i in range(3):
         total += dot_nn(tile_ref[i], halo_tile[i], precision=HIGHEST)
-    for c in to_right + to_left:
-        c.wait()
     keep = (iota((PAD, half), 0) < mid) == (iota((PAD, half), 1) < half // 2)
-    for side, ref in ((0, left_ref), (1, right_ref)):
+    for side, ref in ((1, right_ref), (0, left_ref)):
+        for c in sent[side]:
+            c.wait()
         again = halo_spare[side]
         extra = jnp.where(keep, jnp.concatenate([again, again], axis=0), 0.0)
         high, middle, _ = split3(jnp.concatenate([halo_pair[side], extra], axis=1))
@@ -292,9 +302,9 @@
     half = pixels // 2
     vmem = pl.BlockSpec(memory_space=pltpu.VMEM)
     f32, bf16 = jnp.float32, jnp.bfloat16
-    copies = 2 * CHUNKS + 5
-
-    blocks = phases.transpose(0, 2, 1).reshape(own_ifg, count, pixels).transpose(1, 0, 2)
+    copies = sum(CHUNKS) + 5
+
+    blocks = phases.transpose(0, 2, 1).reshape(own_ifg, count, 2, half).transpose(2, 1, 0, 3)
     padded = jnp.pad(class_weights, ((0, LANES - CLASSES), (0, 0)))
     corrected = pl.pallas_call(
         functools.partial(kernel, tile_rows, tile_cols),
@@ -302,10 +312,10 @@
         in_specs=[vmem] * 5,
         out_specs=vmem,
         scratch_shapes=[
-            pltpu.VMEM((count, own_ifg, pixels), f32),
+            pltpu.VMEM((2, count, own_ifg, half), f32),
             pltpu.VMEM((PAD, nifg), bf16),
             pltpu.VMEM((nifg, pixels), f32),
-            pltpu.VMEM((MAXGAP + 1, PAD, pixels), f32),
+            pltpu.VMEM((2, MAXGAP + 1, PAD, half), f32),
             pltpu.VMEM((MAXGAP + 1, PAD, LANES), f32),
             pltpu.VMEM((MAXGAP + 1, PAD, LANES), f32),
             pltpu.VMEM((pixels, pixels), f32),
@@ -313,16 +323,16 @@
             pltpu.VMEM((2, pixels, pixels), bf16),
             pltpu.VMEM((16, pixels), f32),
             pltpu.VMEM((3, pixels, 16), f32),
-            pltpu.VMEM((PAD + 8, pixels), f32),
-            pltpu.VMEM((PAD, pixels), f32),
+            pltpu.VMEM((PAD + 8, half), f32),
+            pltpu.VMEM((2, PAD, half), f32),
             pltpu.VMEM((2, PAD // 2, half), f32),
             pltpu.VMEM((16, PAD), f32),
             pltpu.VMEM((2, PAD, half), f32),
             pltpu.VMEM((2, PAD // 2, half), f32),
             pltpu.VMEM((3, 16, PAD), f32),
-            pltpu.SemaphoreType.DMA((count,)),
-            pltpu.SemaphoreType.DMA((count,)),
-            pltpu.SemaphoreType.DMA,
+            pltpu.SemaphoreType.DMA((2, count)),
+            pltpu.SemaphoreType.DMA((2, count)),
+            pltpu.SemaphoreType.DMA((2,)),
             pltpu.SemaphoreType.DMA((copies,)),
             pltpu.SemaphoreType.DMA((copies,)),
         ],

time: 51.6 us -> 53.3 us (1.033)
  Pallas kernels: 46.8 us -> 48.1 us
    pallas_call x1, Pallas kernels: 46.8 us -> 48.1 us  [on_device(): pl.pallas_call(functools.partial(kernel, tile_rows, tile_cols), out_shape...]
where the time goes in v3:
time: 53.3 us; the launch traced here: 53.1 us
  Pallas kernels  48.1 us (90%)
  local copies, waits for them, and re-layouts  4.96 us (9%)
    pallas_call x1, Pallas kernels, on_device(): pl.pallas_call(functools.partial(kernel, tile_rows, tile_cols), out_shape...  48.1 us
    transpose x1, local copies, waits for them, and re-layouts, on_device(): phases.transpose(0, 2, 1).reshape(own_ifg, count, 2, half)  1.92 us
    reshape x2, local copies, waits for them, and re-layouts, on_device(): phases.transpose(0, 2, 1).reshape(own_ifg, count, 2, half)  1.63 us

profile of v3, /device:TPU:1, one launch (start us, length us, event | category | flops | bytes accessed | tf_op | source)
XLA Modules:
  0.0 53.1 jit_solution(10964927376687421933)
XLA Ops:
  0.0 1.9 %copy.7 = f32[64,64,64]{2,1,0:T(8,128)S(1)} copy(f32[64,64,64]{1,2,0:T(8,128)} %bitcast.10) | data formatting | bytes 2097152 | tf_op jit(solution)/shard_map/transpose | solution.py:307
  1.9 0.0 copy-start.1
  1.9 1.0 %reshape.9 = f32[64,16,2,128]{3,2,1,0:T(2,128)S(1)} reshape(f32[64,64,64]{2,1,0:T(8,128)S(1)} %copy.7) | data formatting | bytes 2097152 | tf_op jit(solution)/shard_map/reshape | solution.py:307
  3.0 0.0 copy-start.2
  3.0 0.0 copy-start
  3.0 0.6 %copy.13 = f32[64,16,2,128]{3,0,1,2:T(8,128)S(1)} copy(f32[64,16,2,128]{3,2,1,0:T(2,128)S(1)} %reshape.9) | data formatting | bytes 2097152 | tf_op jit(solution)/shard_map/reshape | solution.py:307
  3.6 0.0 copy-done.1
  3.6 0.2 copy.9
  3.8 0.2 copy.12
  4.0 0.1 pad.4.clone.w_ref
  4.1 0.0 copy-done.2
  4.1 0.1 reshape.10.cls_ref
  4.2 0.0 copy-done
  4.2 48.1 %invert_and_filter.1 = f32[256,300]{1,0:T(8,128)S(1)} custom-call(f32[2,16,64,128]{3,2,1,0:T(8,128)S(1)} %bitcast.8, s32[2,1024]{1,0:T(2,128)S(1)} %bitcast.9, f32[128,1024]{1,0:T(8,128)S(1)} %pad.4.clone.w_ref, f32[1024,128]{1,0:T(8,128)S(1)} %pad_bitcast_fusion.wt_ref, s32[1,256]{1,0:T(1,128)S(1)} %reshape.10.cls_ref), custom_call_target="tpu_custom_call" | custom-call | tf_op jit(solution)/shard_map/invert_and_filter/pallas_call | solution.py:309
  52.3 0.9 %reshape.11 = f32[64,4,300]{2,1,0:T(4,128)} reshape(f32[256,300]{1,0:T(8,128)S(1)} %invert_and_filter.1) | data formatting | bytes 614400 | tf_op jit(solution)/shard_map/reshape | solution.py:344
  (1 shorter events, 0.0 us)
Async XLA Ops:
  1.9 1.7 %copy-start.1 = (f32[8,1024]{1,0:T(8,128)S(1)}, f32[8,1024]{1,0:T(8,128)}, u32[]{:S(2)}) copy-start(f32[8,1024]{1,0:T(8,128)} %param.6) | copy-start | bytes 98308
  3.0 1.1 %copy-start.2 = (s32[64,4]{0,1:T(4,128)S(1)}, s32[64,4]{0,1:T(4,128)}, u32[]{:S(2)}) copy-start(s32[64,4]{0,1:T(4,128)} %param.7) | copy-start | bytes 3076
  3.0 1.2 %copy-start = (s32[1024,2]{0,1:T(2,128)S(1)}, s32[1024,2]{0,1:T(2,128)}, u32[]{:S(2)}) copy-start(s32[1024,2]{0,1:T(2,128)} %param.5) | copy-start | bytes 24580

commit v4 on v2

--- a/solution.py
+++ b/solution.py
@@ -240,6 +240,20 @@
                                             recv_sem=recv_sem.at[i], device_id=device,
                                             device_id_type=MESH)
 
+    has_left, has_right = me > 0, me < count - 1
+
+    @pl.when(jnp.logical_not(has_left))
+    def _():
+        halo_pair[0] = jnp.zeros_like(halo_pair[0])
+        halo_spare[0] = jnp.zeros_like(halo_spare[0])
+        halo_tile[0] = jnp.zeros_like(halo_tile[0])
+
+    @pl.when(jnp.logical_not(has_right))
+    def _():
+        halo_pair[1] = jnp.zeros_like(halo_pair[1])
+        halo_spare[1] = jnp.zeros_like(halo_spare[1])
+        halo_tile[2] = jnp.zeros_like(halo_tile[2])
+
     half = pixels // 2
     total_blocks = PAD // 8
     cuts = [total_blocks * (CHUNKS - i) // CHUNKS for i in range(CHUNKS + 1)]
@@ -251,9 +265,17 @@
         span = pl.ds(bottom * 8, (top - bottom) * 8)
         to_left.append(copy(2 * i, x_ref.at[span, pl.ds(0, half)], halo_pair.at[1, span], (left, core)))
         to_right.append(copy(2 * i + 1, x_ref.at[span, pl.ds(half, half)], halo_pair.at[0, span], (right, core)))
-        to_left[-1].start()
-        to_right[-1].start()
+        if i < CHUNKS - 1:
+            pl.when(has_left)(to_left[-1].start)
+            pl.when(has_right)(to_right[-1].start)
     x = x_ref[...]
+    edge[...] = dot_nt(sel_ref[...], x, precision=HIGHEST)
+    small = [copy(2 * CHUNKS + 2 + i, edge, halo_tile.at[slot], near[i]) for i, slot in enumerate((1, 2, 0))]
+    small[0].start()
+    pl.when(has_left)(small[1].start)
+    pl.when(has_right)(small[2].start)
+    pl.when(has_left)(to_left[-1].start)
+    pl.when(has_right)(to_right[-1].start)
     mid = PAD // 2
     low_lanes = iota((mid, half), 1) < half // 2
     first, second = x[:, 0:half], x[:, half:]
@@ -261,19 +283,22 @@
     spare[1] = jnp.where(low_lanes, second[0:mid], pltpu.roll(second[mid:], half // 2, 1))
     to_right.append(copy(2 * CHUNKS, spare.at[0], halo_spare.at[0], (right, core)))
     to_left.append(copy(2 * CHUNKS + 1, spare.at[1], halo_spare.at[1], (left, core)))
-    to_right[-1].start()
-    to_left[-1].start()
-    edge[...] = dot_nt(sel_ref[...], x, precision=HIGHEST)
-    small = [copy(2 * CHUNKS + 2 + i, edge, halo_tile.at[slot], near[i]) for i, slot in enumerate((1, 2, 0))]
-    for c in small:
-        c.start()
+    pl.when(has_right)(to_right[-1].start)
+    pl.when(has_left)(to_left[-1].start)
     total = dot_nt(own_ref[...], x, precision=HIGHEST)
-    for c in small:
-        c.wait()
+    small[0].wait()
+    pl.when(has_left)(small[1].wait_send)
+    pl.when(has_right)(small[1].wait_recv)
+    pl.when(has_right)(small[2].wait_send)
+    pl.when(has_left)(small[2].wait_recv)
     for i in range(3):
         total += dot_nn(tile_ref[i], halo_tile[i], precision=HIGHEST)
-    for c in to_right + to_left:
-        c.wait()
+    for c in to_right:
+        pl.when(has_right)(c.wait_send)
+        pl.when(has_left)(c.wait_recv)
+    for c in to_left:
+        pl.when(has_left)(c.wait_send)
+        pl.when(has_right)(c.wait_recv)
     keep = (iota((PAD, half), 0) < mid) == (iota((PAD, half), 1) < half // 2)
     for side, ref in ((0, left_ref), (1, right_ref)):
         again = halo_spare[side]

time: 51.6 us -> 49.3 us (0.955)
  the two profiles are of different devices: /device:TPU:1 before, /device:TPU:10 now
where the time goes in v4:
time: 49.3 us; the launch traced here: 49.2 us
  Pallas kernels  44.6 us (90%)
  local copies, waits for them, and re-layouts  4.47 us (9%)
    pallas_call x1, Pallas kernels, on_device(): pl.pallas_call(functools.partial(kernel, tile_rows, tile_cols), out_shape...  44.6 us
    transpose x1, local copies, waits for them, and re-layouts, on_device(): phases.transpose(0, 2, 1).reshape(own_ifg, count, pixels).transpose(1, 0, 2)  1.92 us
    reshape x2, local copies, waits for them, and re-layouts, on_device(): phases.transpose(0, 2, 1).reshape(own_ifg, count, pixels).transpose(1, 0, 2)  1.14 us

profile of v4, /device:TPU:10, one launch (start us, length us, event | category | flops | bytes accessed | tf_op | source)
XLA Modules:
  0.0 49.2 jit_solution(866153840382863962)
XLA Ops:
  0.0 1.9 %copy.7 = f32[64,64,64]{2,1,0:T(8,128)S(1)} copy(f32[64,64,64]{1,2,0:T(8,128)} %bitcast.10) | data formatting | bytes 2097152 | tf_op jit(solution)/shard_map/transpose | solution.py:322
  1.9 0.0 copy-start.1
  1.9 0.5 %reshape.9 = f32[64,16,256]{2,1,0:T(8,128)S(1)} reshape(f32[64,64,64]{2,1,0:T(8,128)S(1)} %copy.7) | data formatting | bytes 2097152 | tf_op jit(solution)/shard_map/reshape | solution.py:322
  2.5 0.0 copy-start.2
  2.5 0.0 copy-start
  2.5 0.6 %copy.13 = f32[64,16,256]{2,0,1:T(8,128)S(1)} copy(f32[64,16,256]{2,1,0:T(8,128)S(1)} %reshape.9) | data formatting | bytes 2097152 | tf_op jit(solution)/shard_map/reshape | solution.py:322
  3.1 0.0 copy-done.1
  3.1 0.2 copy.9
  3.3 0.2 copy.12
  3.5 0.1 pad.4.clone.w_ref
  3.6 0.0 copy-done.2
  3.6 0.1 reshape.10.cls_ref
  3.7 0.0 copy-done
  3.7 44.6 %invert_and_filter.1 = f32[256,300]{1,0:T(8,128)S(1)} custom-call(f32[16,64,256]{2,1,0:T(8,128)S(1)} %bitcast.8, s32[2,1024]{1,0:T(2,128)S(1)} %bitcast.9, f32[128,1024]{1,0:T(8,128)S(1)} %pad.4.clone.w_ref, f32[1024,128]{1,0:T(8,128)S(1)} %pad_bitcast_fusion.wt_ref, s32[1,256]{1,0:T(1,128)S(1)} %reshape.10.cls_ref), custom_call_target="tpu_custom_call" | custom-call | tf_op jit(solution)/shard_map/invert_and_filter/pallas_call | solution.py:324
  48.3 0.9 %reshape.11 = f32[64,4,300]{2,1,0:T(4,128)} reshape(f32[256,300]{1,0:T(8,128)S(1)} %invert_and_filter.1) | data formatting | bytes 614400 | tf_op jit(solution)/shard_map/reshape | solution.py:359
  (1 shorter events, 0.0 us)
Async XLA Ops:
  1.9 1.2 %copy-start.1 = (f32[8,1024]{1,0:T(8,128)S(1)}, f32[8,1024]{1,0:T(8,128)}, u32[]{:S(2)}) copy-start(f32[8,1024]{1,0:T(8,128)} %param.6) | copy-start | bytes 98308
  2.5 1.1 %copy-start.2 = (s32[64,4]{0,1:T(4,128)S(1)}, s32[64,4]{0,1:T(4,128)}, u32[]{:S(2)}) copy-start(s32[64,4]{0,1:T(4,128)} %param.7) | copy-start | bytes 3076
  2.5 1.2 %copy-start = (s32[1024,2]{0,1:T(2,128)S(1)}, s32[1024,2]{0,1:T(2,128)}, u32[]{:S(2)}) copy-start(s32[1024,2]{0,1:T(2,128)} %param.5) | copy-start | bytes 24580

commit v5 on v4

--- a/solution.py
+++ b/solution.py
@@ -149,13 +149,13 @@
     sel_c, sel_r = split_index(iota((16, pixels), 1), tile_rows)
     sent_r = jnp.where(core == 0, tile_rows - R, 0) + slot_j
     sel_ref[...] = jnp.where((slot_j < R) & (sent_r == sel_r) & (slot_c == sel_c), 1.0, 0.0)
-    slot_c, slot_j = split_index(iota((pixels, 16), 1), 4)
-    out_r, out_c = split_index(iota((pixels, 16), 0), tile_cols)
+    side, slot = split_index(iota((pixels, 48), 1), 16)
+    slot_c, slot_j = split_index(slot, 4)
+    out_r, out_c = split_index(iota((pixels, 48), 0), tile_cols)
     got_r = jnp.where(core == 0, tile_rows, -R) + slot_j
     reach = jnp.where(slot_j < R, tap(out_r - got_r), 0.0)
-    tile_ref[0] = -has_left * reach * tap(out_c - slot_c + tile_cols)
-    tile_ref[1] = -reach * tap(out_c - slot_c)
-    tile_ref[2] = -has_right * reach * tap(out_c - slot_c - tile_cols)
+    has = jnp.where(side == 0, has_left, jnp.where(side == 1, 1.0, has_right))
+    tile_ref[...] = -has * reach * tap(out_c - slot_c + (1 - side) * tile_cols)
 
 
 def kernel(tile_rows, tile_cols, blocks_ref, pairs_ref, w_ref, wt_ref, cls_ref, out_ref,
@@ -291,8 +291,7 @@
     pl.when(has_right)(small[1].wait_recv)
     pl.when(has_right)(small[2].wait_send)
     pl.when(has_left)(small[2].wait_recv)
-    for i in range(3):
-        total += dot_nn(tile_ref[i], halo_tile[i], precision=HIGHEST)
+    total += dot_nn(tile_ref[...], halo_tile[...].reshape(48, PAD), precision=HIGHEST)
     for c in to_right:
         pl.when(has_right)(c.wait_send)
         pl.when(has_left)(c.wait_recv)
@@ -337,7 +336,7 @@
             pltpu.VMEM((2, pixels, pixels), bf16),
             pltpu.VMEM((2, pixels, pixels), bf16),
             pltpu.VMEM((16, pixels), f32),
-            pltpu.VMEM((3, pixels, 16), f32),
+            pltpu.VMEM((pixels, 48), f32),
             pltpu.VMEM((PAD + 8, pixels), f32),
             pltpu.VMEM((PAD, pixels), f32),
             pltpu.VMEM((2, PAD // 2, half), f32),

time: 49.3 us -> 49.1 us (level)
  no operation moved by 1% of the time
where the time goes in v5:
time: 49.1 us; the launch traced here: 49 us
  Pallas kernels  44.4 us (90%)
  local copies, waits for them, and re-layouts  4.47 us (9%)
    pallas_call x1, Pallas kernels, on_device(): pl.pallas_call(functools.partial(kernel, tile_rows, tile_cols), out_shape...  44.4 us
    transpose x1, local copies, waits for them, and re-layouts, on_device(): phases.transpose(0, 2, 1).reshape(own_ifg, count, pixels).transpose(1, 0, 2)  1.92 us
    reshape x2, local copies, waits for them, and re-layouts, on_device(): phases.transpose(0, 2, 1).reshape(own_ifg, count, pixels).transpose(1, 0, 2)  1.14 us

profile of v5, /device:TPU:10, one launch (start us, length us, event | category | flops | bytes accessed | tf_op | source)
XLA Modules:
  0.0 49.0 jit_solution(1743462845240308741)
XLA Ops:
  0.0 1.9 %copy.7 = f32[64,64,64]{2,1,0:T(8,128)S(1)} copy(f32[64,64,64]{1,2,0:T(8,128)} %bitcast.10) | data formatting | bytes 2097152 | tf_op jit(solution)/shard_map/transpose | solution.py:321
  1.9 0.0 copy-start.1
  1.9 0.5 %reshape.9 = f32[64,16,256]{2,1,0:T(8,128)S(1)} reshape(f32[64,64,64]{2,1,0:T(8,128)S(1)} %copy.7) | data formatting | bytes 2097152 | tf_op jit(solution)/shard_map/reshape | solution.py:321
  2.5 0.0 copy-start.2
  2.5 0.0 copy-start
  2.5 0.6 %copy.13 = f32[64,16,256]{2,0,1:T(8,128)S(1)} copy(f32[64,16,256]{2,1,0:T(8,128)S(1)} %reshape.9) | data formatting | bytes 2097152 | tf_op jit(solution)/shard_map/reshape | solution.py:321
  3.1 0.0 copy-done.1
  3.1 0.2 copy.9
  3.3 0.2 copy.12
  3.5 0.1 pad.4.clone.w_ref
  3.6 0.0 copy-done.2
  3.6 0.1 reshape.10.cls_ref
  3.7 0.0 copy-done
  3.7 44.4 %invert_and_filter.1 = f32[256,300]{1,0:T(8,128)S(1)} custom-call(f32[16,64,256]{2,1,0:T(8,128)S(1)} %bitcast.8, s32[2,1024]{1,0:T(2,128)S(1)} %bitcast.9, f32[128,1024]{1,0:T(8,128)S(1)} %pad.4.clone.w_ref, f32[1024,128]{1,0:T(8,128)S(1)} %pad_bitcast_fusion.wt_ref, s32[1,256]{1,0:T(1,128)S(1)} %reshape.10.cls_ref), custom_call_target="tpu_custom_call" | custom-call | tf_op jit(solution)/shard_map/invert_and_filter/pallas_call | solution.py:323
  48.1 0.9 %reshape.11 = f32[64,4,300]{2,1,0:T(4,128)} reshape(f32[256,300]{1,0:T(8,128)S(1)} %invert_and_filter.1) | data formatting | bytes 614400 | tf_op jit(solution)/shard_map/reshape | solution.py:358
  (1 shorter events, 0.0 us)
Async XLA Ops:
  1.9 1.2 %copy-start.1 = (f32[8,1024]{1,0:T(8,128)S(1)}, f32[8,1024]{1,0:T(8,128)}, u32[]{:S(2)}) copy-start(f32[8,1024]{1,0:T(8,128)} %param.6) | copy-start | bytes 98308
  2.5 1.1 %copy-start.2 = (s32[64,4]{0,1:T(4,128)S(1)}, s32[64,4]{0,1:T(4,128)}, u32[]{:S(2)}) copy-start(s32[64,4]{0,1:T(4,128)} %param.7) | copy-start | bytes 3076
  2.5 1.2 %copy-start = (s32[1024,2]{0,1:T(2,128)S(1)}, s32[1024,2]{0,1:T(2,128)}, u32[]{:S(2)}) copy-start(s32[1024,2]{0,1:T(2,128)} %param.5) | copy-start | bytes 24580
